TPU v7x, 256 devices: a whole 4x4x8 slice. The times are simulated.
256 devices in a mesh: space: 16 (over y_lo, x, core), tm: 16 (over z, y_hi).
Axes of the slice: x: 4, y: 4 (y_hi: 2, y_lo: 2; y = y_hi * 2 + y_lo), z: 8, core: 2. Of those that a mesh axis runs over, the one named last changes fastest.
Arguments:
- record: float32 [3072, 65536], P('tm', 'space'), may hold values from -40 to 40
- mode_basis: float32 [21, 48, 48], replicated, may hold values from -0.2 to 1.2
- slow_picks: int32 [21, 32], replicated, may hold values from 0 to 47, all different within a row
- phases: int32 [21], replicated, may hold values from 0 to 3
Outputs:
- residual_record: float32 [3072, 65536], P('tm', 'space')
Inputs may be any that keep to these rules, and one draw needn't show every extreme that they name: `slow_picks`: the 32 entries of a row are different.
All inputs are finite; a program needn't handle non-finite values.
Results may differ from a plain program's by a relative error of at most 0.003.
Values may be sent and summed in bfloat16 or wider, within the bound.
A program may use at most 64 MiB of HBM per device.

v0:
```python
import jax
import jax.numpy as jnp
from jax import lax
from jax.sharding import PartitionSpec as P

precise = lax.Precision.HIGHEST


def choose_columns(basis_w, picks_w, gram, points):
    size_m = basis_w.shape[1]
    modes_r = picks_w.shape[1]
    onehot = (picks_w[:, :, None] == jnp.arange(size_m, dtype=jnp.int32)[None, None, :]).astype(
        jnp.float32
    )
    chosen = jnp.einsum("wmn,wrn->wmr", basis_w, onehot, precision=precise)
    inner = jnp.einsum("wmn,wnr->wmr", gram, chosen, precision=precise)
    kernel = (
        jnp.einsum("wmr,wms->wrs", chosen, inner, precision=precise)
        + 1e-05 * jnp.eye(modes_r, dtype=jnp.float32)[None]
    )
    factor = jnp.linalg.cholesky(kernel)
    solved = lax.linalg.triangular_solve(
        factor, chosen, left_side=False, lower=True, transpose_a=True
    )
    return solved / jnp.sqrt(jnp.asarray(points, jnp.float32))


def project(modes, segments):
    partial_amp = jnp.einsum("wrp,wtp->wrt", modes, segments, precision=precise)
    return lax.psum(partial_amp, "space")


def remove_slow(segments, amplitude, modes):
    return segments - jnp.einsum("wrt,wrp->wtp", amplitude, modes, precision=precise)


def local_level(samples, basis_w, picks_w, segments, points):
    widened = samples.astype(jnp.float32)
    gram_part = jnp.einsum("wmp,wnp->wmn", samples, samples, preferred_element_type=jnp.float32)
    gram_total = lax.psum(gram_part, "space")
    weights = choose_columns(basis_w, picks_w, gram_total / points, points)
    modes = jnp.einsum("wmr,wmp->wrp", weights, widened, precision=precise)
    amplitude = project(modes, segments)
    return remove_slow(segments, amplitude, modes)


def body(record, mode_basis, slow_picks, phases):
    steps_dev, points_dev = record.shape
    size_m = mode_basis.shape[1]
    time_groups = lax.axis_size("tm")
    points = points_dev * lax.axis_size("space")
    position = lax.axis_index("tm")
    field = record
    offset_base = 0
    for level in range(3):
        window_count = 4**level
        stride = steps_dev * time_groups // (window_count * size_m)
        segment_count = max(1, window_count // time_groups)
        seglen = steps_dev // segment_count
        if window_count >= time_groups:
            first_win = position * segment_count
        else:
            first_win = position // (time_groups // window_count)
        owned_ids = first_win + jnp.arange(segment_count, dtype=jnp.int32)
        level_phases = phases[offset_base : offset_base + window_count]
        matches = (owned_ids[:, None] == jnp.arange(window_count, dtype=jnp.int32)[None, :]).astype(
            jnp.int32
        )
        offsets = jnp.sum(matches * level_phases[None, :], axis=1) % stride
        select = (jnp.arange(stride, dtype=jnp.int32)[None, :] == offsets[:, None]).astype(
            jnp.float32
        )
        shaped = field.reshape(segment_count, seglen // stride, stride, points_dev)
        sampled = jnp.sum(shaped * select[:, None, :, None], axis=2).astype(jnp.bfloat16)
        segments = field.reshape(segment_count, seglen, points_dev)
        level_basis = mode_basis[offset_base : offset_base + window_count]
        level_picks = slow_picks[offset_base : offset_base + window_count]
        if window_count >= time_groups:
            basis_w = lax.dynamic_slice_in_dim(level_basis, first_win, segment_count, 0)
            picks_w = lax.dynamic_slice_in_dim(level_picks, first_win, segment_count, 0)
            field = local_level(sampled, basis_w, picks_w, segments, points).reshape(
                steps_dev, points_dev
            )
        else:
            gathered = lax.all_gather(sampled[0], "tm", axis=0, tiled=True)
            own_rows = lax.dynamic_slice_in_dim(gathered, first_win * size_m, size_m, 0)[None]
            basis_w = lax.dynamic_slice_in_dim(level_basis, first_win, 1, 0)
            picks_w = lax.dynamic_slice_in_dim(level_picks, first_win, 1, 0)
            field = local_level(own_rows, basis_w, picks_w, segments, points).reshape(
                steps_dev, points_dev
            )
        offset_base = offset_base + window_count
    return field


def solution(mesh):
    in_specs = (P("tm", "space"), P(), P(), P())
    out_specs = P("tm", "space")
    return jax.shard_map(body, mesh=mesh, in_specs=in_specs, out_specs=out_specs, check_vma=False)
```

profile of v0, /device:TPU:1, one launch (start us, length us, event | category | flops | bytes accessed | tf_op | source)
XLA Modules:
  0.0 553.5 jit_solution(532614290910513424)
XLA Ops:
  7.2 1.4 fusion.58
  10.6 2.4 multiply_reduce_fusion.2
  13.0 43.0 %all-gather = bf16[16,3,4096]{2,1,0:T(4,128)(2,1)} all-gather(bf16[1,3,4096]{2,1,0:T(4,128)(2,1)S(1)} %bitcast.166), channel_id=1, replica_groups=mesh['space'=16,'tm'=16] {'tm'}, dimensions={0}, use_global_device_ids=true | all-gather | bytes 417792 | tf_op jit(solution)/shard_map/all_gather | solution.py:85
  56.0 1.4 reshape.499
  57.3 0.9 convolution_bitcast_fusion.2
  58.2 56.2 %psum.42 = f32[1,48,48]{2,1,0:T(8,128)} all-reduce(f32[1,48,48]{2,1,0:T(8,128)} %convolution_bitcast_fusion.2), channel_id=1, replica_groups=mesh['space'=16,'tm'=16] {'space'}, use_global_device_ids=true, to_apply=%region_1.2 | all-reduce | flops 2304 | bytes 18432 | tf_op jit(solution)/shard_map/psum | solution.py:40
  115.0 0.9 fusion.22
  116.0 0.9 fusion.20
  116.9 0.8 convolution_add_fusion.2
  117.6 1.4 copy.18
  119.0 1.3 fusion.36
  120.4 4.2 custom-call.10
  126.0 1.9 fusion.30
  127.9 3.8 custom-call.11
  131.6 0.9 fusion.1
  133.0 0.8 copy-done.3
  133.7 2.9 fusion.64
  136.7 52.9 %psum.43 = f32[32,192]{1,0:T(8,128)S(1)} all-reduce(f32[32,192]{1,0:T(8,128)S(1)} %fusion.64), channel_id=1, replica_groups=mesh['space'=16,'tm'=16] {'space'}, use_global_device_ids=true, to_apply=%region_4.7 | all-reduce | flops 6144 | bytes 49152 | tf_op jit(solution)/shard_map/psum | solution.py:30
  189.6 4.7 convolution_subtract_fusion.2
  194.4 1.3 multiply_reduce_fusion.1
  198.4 1.8 slice.42
  200.9 0.9 fusion.14
  201.8 74.3 %all-gather.4.cloned.1.call-done = bf16[16,12,4096]{2,1,0:T(8,128)(2,1)} async-done(((bf16[1,12,4096]{2,1,0:T(8,128)(2,1)}), bf16[16,12,4096]{2,1,0:T(8,128)(2,1)}) %all-gather.4.cloned.1.call-update) | async-done | bytes 1572880 | tf_op jit(solution)/shard_map/all_gather | solution.py:85
  276.1 3.6 reshape.501
  279.6 1.4 convolution_bitcast_fusion.1
  281.0 52.9 %psum.44 = f32[1,48,48]{2,1,0:T(8,128)S(1)} all-reduce(f32[1,48,48]{2,1,0:T(8,128)S(1)} %convolution_bitcast_fusion.1), channel_id=1, replica_groups=mesh['space'=16,'tm'=16] {'space'}, use_global_device_ids=true, to_apply=%region_7.10 | all-reduce | flops 2304 | bytes 18432 | tf_op jit(solution)/shard_map/psum | solution.py:40
  334.3 2.9 custom-call.12
  338.7 2.4 custom-call.13
  341.4 1.4 fusion.6
  342.7 0.8 copy-done.4
  343.5 2.9 fusion.65
  346.5 52.9 %psum.45 = f32[32,192]{1,0:T(8,128)S(1)} all-reduce(f32[32,192]{1,0:T(8,128)S(1)} %fusion.65), channel_id=1, replica_groups=mesh['space'=16,'tm'=16] {'space'}, use_global_device_ids=true, to_apply=%region_8.11 | all-reduce | flops 6144 | bytes 49152 | tf_op jit(solution)/shard_map/psum | solution.py:30
  399.4 5.4 convolution_subtract_fusion.1
  404.7 4.8 reshape_reshape.7
  409.5 4.2 multiply_reduce_fusion
  413.7 0.8 convolution_bitcast_fusion
  414.6 53.1 %psum.46 = f32[1,48,48]{2,1,0:T(8,128)} all-reduce(f32[1,48,48]{2,1,0:T(8,128)} %convolution_bitcast_fusion), channel_id=1, replica_groups=mesh['space'=16,'tm'=16] {'space'}, use_global_device_ids=true, to_apply=%region_11.14 | all-reduce | flops 2304 | bytes 18432 | tf_op jit(solution)/shard_map/psum | solution.py:40
  467.7 0.9 fusion.12
  469.4 1.4 copy.22
  470.8 1.3 fusion.33
  472.1 4.2 custom-call.14
  477.7 1.9 fusion.32
  479.6 3.8 custom-call.15
  483.4 0.9 fusion.5
  484.7 0.8 copy-done.2
  485.5 2.9 fusion.66
  488.4 52.9 %psum.47 = f32[32,192]{1,0:T(8,128)S(1)} all-reduce(f32[32,192]{1,0:T(8,128)S(1)} %fusion.66), channel_id=1, replica_groups=mesh['space'=16,'tm'=16] {'space'}, use_global_device_ids=true, to_apply=%region_12.15 | all-reduce | flops 6144 | bytes 49152 | tf_op jit(solution)/shard_map/psum | solution.py:30
  541.3 5.4 convolution_subtract_fusion
  (40 shorter events, 8.4 us)
Async XLA Ops:
  6.5 269.5 %all-gather.4.cloned.1.call-start = ((), (), s32[]{:S(2)}) async-start(), calls=%async_computation | async-start | bytes 2228224 | tf_op jit(solution)/shard_map/all_gather | solution.py:85
  10.6 123.2 %copy-start.1 = (f32[192,4096]{1,0:T(8,128)S(1)}, f32[192,4096]{1,0:T(8,128)}, u32[]{:S(2)}) copy-start(f32[192,4096]{1,0:T(8,128)} %param.7) | copy-start | bytes 9437188
  132.9 0.8 copy-start.3
  194.3 1.4 copy-start.5
  194.3 1.4 copy-start.6
  194.3 6.3 %slice-start = ((f32[21,48,48]{2,1,0:T(8,128)}), f32[4,48,48]{2,1,0:T(8,128)S(1)}, s32[]{:S(2)}) async-start(f32[21,48,48]{2,1,0:T(8,128)} %param.8), calls=%async_computation.1 | async-start | bytes 196608 | tf_op jit(solution)/shard_map/slice | solution.py:76
  342.7 0.8 copy-start.4
  409.5 75.9 %copy-start = (f32[192,4096]{1,0:T(8,128)S(1)}, f32[192,4096]{1,0:T(8,128)}, u32[]{:S(2)}) copy-start(f32[192,4096]{1,0:T(8,128)} %convolution_subtract_fusion.1) | copy-start | bytes 9437188
  484.7 0.8 copy-start.2
Sparse Core Ops, SparseCore 0:
  195.8 80.1 all-gather.3
where the time goes:
time: 559 us; the launch traced here: 554 us
  blocking collectives  364 us (65%)
  waiting for transfers between devices  74.3 us (13%)
  other arithmetic  42.5 us (8%)
  matrix products  37.1 us (7%)
  between operations  18.3 us (3%)
  local copies, waits for them, and re-layouts  17.4 us (3%)
    psum x3, blocking collectives, local_level(): gram_total = lax.psum(gram_part, 'space')  162 us
    psum x3, blocking collectives, project(): return lax.psum(partial_amp, 'space')  159 us
    all_gather x1, waiting for transfers between devices, body(): gathered = lax.all_gather(sampled[0], 'tm', axis=0, tiled=True)  74.3 us
    all_gather x1, blocking collectives, body(): gathered = lax.all_gather(sampled[0], 'tm', axis=0, tiled=True)  43 us
    dot_general x3, matrix products, remove_slow(): jnp.einsum('wrt,wrp->wtp', amplitude, modes, precision=precise)  15.4 us
    another operation x9, other arithmetic, choose_columns(): factor = jnp.linalg.cholesky(kernel)  14.9 us
    another operation x6, other arithmetic, choose_columns(): lax.linalg.triangular_solve(factor, chosen, left_side=False, lower=True,...  14.5 us
  transfers between devices with their start and end apart: 1, of which 1 were waited for; matrix products, arithmetic and copies ran while one was open for 1% of the time, Pallas kernels for 0%

commit v1 on v0

v1 whole, which is shorter than its diff:
```python
import functools

import jax
import jax.numpy as jnp
from jax import lax
from jax.experimental import pallas as pl
from jax.experimental.pallas import tpu as pltpu
from jax.sharding import PartitionSpec as P

M = 48
R = 32
LEVELS = 3
SEG = 128
WIDTH = 512
EPS = 1e-5
MESH = pl.DeviceIdType.MESH
EXACT = lax.Precision.HIGHEST
VMEM_LIMIT = 56 * 1024 * 1024


def dot_nt(a, b):
    return lax.dot_general(a, b, (((1,), (1,)), ((), ())), preferred_element_type=jnp.float32)


def exact(a, b):
    return jnp.dot(a, b, precision=EXACT, preferred_element_type=jnp.float32)


def collect(
    nt, ns, owners,
    phases, picks, basis_hbm, record,
    y_out, sums_out, chosen_out,
    field, split, y, outbox, got0, got1, wide, basis, chosen, cross, own_gram, part, inbox, total,
    load_sem, basis_sem, send0_sem, recv0_sem, send1_sem, recv1_sem, sendr_sem, recvr_sem, senda_sem, recva_sem,
):
    steps, points = record.shape
    segs = points // SEG
    me_t = lax.axis_index("tm")
    me_s = lax.axis_index("space")
    group = nt // 4
    first = me_t // group * group
    rows0 = M // nt
    rows1 = M // group
    span = LEVELS * R // owners

    loads = [
        pltpu.make_async_copy(
            record.at[:, j * SEG : (j + 1) * SEG], field.at[pl.ds(j * steps, steps)], load_sem.at[j]
        )
        for j in range(segs)
    ]
    for load in loads:
        load.start()
    q1 = 1 + me_t // group
    q2 = 5 + me_t
    fetches = [
        pltpu.make_async_copy(basis_hbm.at[q], basis.at[level], basis_sem.at[level])
        for level, q in enumerate((0, q1, q2))
    ]
    for fetch in fetches:
        fetch.start()

    barrier = pltpu.get_barrier_semaphore()
    for d in range(1, nt):
        pl.semaphore_signal(barrier, inc=1, device_id={"tm": lax.rem(me_t + d, nt)}, device_id_type=MESH)
    for d in range(1, ns):
        pl.semaphore_signal(barrier, inc=1, device_id={"space": lax.rem(me_s + d, ns)}, device_id_type=MESH)

    for load in loads:
        load.wait()
    off0 = lax.rem(phases[0], steps * nt // M)
    off1 = lax.rem(phases[q1], steps * group // M)
    off2 = lax.rem(phases[q2], steps // M)
    stride0 = steps * nt // M
    stride1 = steps * group // M
    stride2 = steps // M

    for r in range(rows0):
        outbox[r * segs : (r + 1) * segs] = field[pl.ds(off0 + stride0 * r, segs, stride=steps), :].astype(
            jnp.bfloat16
        )
    for r in range(rows0, rows0 + rows1):
        outbox[r * segs : (r + 1) * segs] = field[
            pl.ds(off1 + stride1 * (r - rows0), segs, stride=steps), :
        ].astype(jnp.bfloat16)
    got0[me_t] = outbox[: rows0 * segs]
    got1[me_t - first] = outbox[rows0 * segs :]

    pl.semaphore_wait(barrier, nt - 1 + ns - 1)

    sends = []
    for d in range(1, group):
        tgt = first + lax.rem(me_t - first + d, group)
        sends.append(
            pltpu.make_async_remote_copy(
                src_ref=outbox.at[pl.ds(rows0 * segs, rows1 * segs)], dst_ref=got1.at[me_t - first],
                send_sem=send1_sem.at[d], recv_sem=recv1_sem.at[me_t - first],
                device_id={"tm": tgt}, device_id_type=MESH,
            )
        )
    for d in range(1, nt):
        tgt = lax.rem(me_t + d, nt)
        sends.append(
            pltpu.make_async_remote_copy(
                src_ref=outbox.at[pl.ds(0, rows0 * segs)], dst_ref=got0.at[me_t],
                send_sem=send0_sem.at[d], recv_sem=recv0_sem.at[me_t],
                device_id={"tm": tgt}, device_id_type=MESH,
            )
        )
    for copy in sends:
        copy.start()

    def part_columns(c, carry):
        cols = pl.ds(pl.multiple_of(c * SEG, SEG), SEG)
        block = field[pl.ds(pl.multiple_of(c * steps, steps), steps), :]
        high = block.astype(jnp.bfloat16)
        split[:steps, cols] = high
        split[steps:, cols] = (block - high.astype(jnp.float32)).astype(jnp.bfloat16)
        x2 = field[pl.ds(c * steps + off2, M, stride=stride2), :]
        high2 = x2.astype(jnp.bfloat16)
        y[2 * M : 3 * M, cols] = high2
        y[3 * M :, cols] = (x2 - high2.astype(jnp.float32)).astype(jnp.bfloat16)
        return carry

    lax.fori_loop(0, segs, part_columns, 0)

    for fetch in fetches:
        fetch.wait()
    lanes = lax.broadcasted_iota(jnp.int32, (M, LEVELS * R), 1)
    rows_m = lax.broadcasted_iota(jnp.int32, (M, LEVELS * R), 0)
    p012 = jnp.concatenate([picks[pl.ds(q, 1), :] for q in (0, q1, q2)], axis=1)
    for level in range(LEVELS):
        hit = (rows_m == p012) & (lanes >= R * level) & (lanes < R * (level + 1))
        chosen[M * level : M * (level + 1)] = exact(basis[level], hit.astype(jnp.float32))
    chosen[LEVELS * M :] = chosen[(LEVELS - 1) * M : LEVELS * M]

    for d in range(1, group):
        src = lax.rem(me_t - first + d, group)
        pltpu.make_async_remote_copy(
            src_ref=outbox.at[pl.ds(rows0 * segs, rows1 * segs)], dst_ref=got1.at[src],
            send_sem=send1_sem.at[d], recv_sem=recv1_sem.at[src],
            device_id={"tm": first + src}, device_id_type=MESH,
        ).wait_recv()
    wide[...] = got1[...].reshape(M * segs, SEG).astype(jnp.float32)
    for j in range(segs):
        y[M : 2 * M, j * SEG : (j + 1) * SEG] = wide[pl.ds(j, M, stride=segs), :].astype(jnp.bfloat16)
    for d in range(1, nt):
        src = lax.rem(me_t + d, nt)
        pltpu.make_async_remote_copy(
            src_ref=outbox.at[pl.ds(0, rows0 * segs)], dst_ref=got0.at[src],
            send_sem=send0_sem.at[d], recv_sem=recv0_sem.at[src],
            device_id={"tm": src}, device_id_type=MESH,
        ).wait_recv()
    wide[...] = got0[...].reshape(M * segs, SEG).astype(jnp.float32)
    for j in range(segs):
        y[:M, j * SEG : (j + 1) * SEG] = wide[pl.ds(j, M, stride=segs), :].astype(jnp.bfloat16)

    cross[...] = jnp.zeros_like(cross)
    own_gram[...] = jnp.zeros_like(own_gram)

    def products(c, carry):
        cols = pl.ds(pl.multiple_of(c * WIDTH, WIDTH), WIDTH)
        rows = y[:, cols]
        cross[...] += dot_nt(rows, split[:steps, cols]) + dot_nt(rows, split[steps:, cols])
        own_gram[...] += dot_nt(rows, rows)
        return carry

    lax.fori_loop(0, points // WIDTH, products, 0)
    turned = chosen[...].T
    part[:, 256:] = jnp.zeros_like(part[:, 256:])
    part[:, 192:256] = jnp.zeros_like(part[:, 192:256])
    part[:, :steps] = exact(turned, cross[...])
    part[:, 256 : 256 + LEVELS * R] = exact(exact(turned, own_gram[...]), chosen[...])

    sums = []
    for d in range(1, ns):
        tgt = lax.rem(me_s + d, ns)
        safe = lax.rem(tgt, owners)
        copy = pltpu.make_async_remote_copy(
            src_ref=part.at[pl.ds(pl.multiple_of(safe * span, span), span)], dst_ref=inbox.at[me_s],
            send_sem=sendr_sem.at[d], recv_sem=recvr_sem.at[me_s],
            device_id={"space": tgt}, device_id_type=MESH,
        )
        sums.append((tgt, copy))
        pl.when(tgt < owners)(copy.start)

    mine = pl.ds(pl.multiple_of(lax.rem(me_s, owners) * span, span), span)
    hands = [
        pltpu.make_async_remote_copy(
            src_ref=total.at[mine], dst_ref=total.at[mine],
            send_sem=senda_sem.at[d], recv_sem=recva_sem.at[me_s],
            device_id={"space": lax.rem(me_s + d, ns)}, device_id_type=MESH,
        )
        for d in range(1, ns)
    ]

    @pl.when(me_s < owners)
    def _():
        acc = part[mine, :]
        for d in range(1, ns):
            src = lax.rem(me_s + d, ns)
            pltpu.make_async_remote_copy(
                src_ref=part.at[mine], dst_ref=inbox.at[src],
                send_sem=sendr_sem.at[d], recv_sem=recvr_sem.at[src],
                device_id={"space": src}, device_id_type=MESH,
            ).wait_recv()
            acc = acc + inbox[src]
        total[mine, :] = acc
        for hand in hands:
            hand.start()

    y_out[...] = y[...]
    chosen_out[...] = chosen[...]

    for d in range(1, ns):
        src = lax.rem(me_s + d, ns)
        theirs = pl.ds(pl.multiple_of(lax.rem(src, owners) * span, span), span)
        arrival = pltpu.make_async_remote_copy(
            src_ref=total.at[mine], dst_ref=total.at[theirs],
            send_sem=senda_sem.at[d], recv_sem=recva_sem.at[src],
            device_id={"space": src}, device_id_type=MESH,
        )
        pl.when(src < owners)(arrival.wait_recv)
    sums_out[...] = total[...]

    for copy in sends:
        copy.wait_send()
    for tgt, copy in sums:
        pl.when(tgt < owners)(copy.wait_send)

    @pl.when(me_s < owners)
    def _():
        for hand in hands:
            hand.wait_send()


def eliminate(block, pivot_lane):
    parts = [block[8 * g : 8 * (g + 1)] for g in range(R // 8)]
    sub = lax.broadcasted_iota(jnp.int32, parts[0].shape, 0)
    for k in range(R):
        g, i = divmod(k, 8)
        lane = pivot_lane + k
        pivot_row = parts[g][i : i + 1, :] / parts[g][i : i + 1, lane : lane + 1]
        fresh = []
        for h in range(R // 8):
            moved = parts[h] - parts[h][:, lane : lane + 1] * pivot_row
            fresh.append(jnp.where(sub == i, pivot_row, moved) if h == g else moved)
        parts = fresh
    return jnp.concatenate(parts, axis=0)


def update(points_all, sums, chosen, y, record, out_hbm, field, out, weights, load_sem, store_sem):
    steps, points = record.shape
    load = pltpu.make_async_copy(record, field, load_sem)
    load.start()
    blocks = [sums[R * level : R * (level + 1), :] / points_all for level in range(LEVELS)]
    lane = lax.broadcasted_iota(jnp.int32, blocks[0].shape, 1)
    row = lax.broadcasted_iota(jnp.int32, blocks[0].shape, 0)
    unit = (lane == steps + row).astype(jnp.float32)
    solved = []
    for level in range(LEVELS):
        at = 256 + R * level
        block = blocks[level]
        ridge = jnp.where(lane == at + row, block + EPS, block) + unit
        done = eliminate(ridge, at)
        inverse = done[:, steps : steps + R]
        done = jnp.where((lane >= at) & (lane < at + R), exact(inverse, block), done)
        solved.append(done)
        if level < LEVELS - 1:
            twice = done + EPS * exact(inverse, done)
            for later in range(level + 1, LEVELS):
                blocks[later] = blocks[later] - exact(blocks[later][:, at : at + R], twice)
                blocks[later] = jnp.where((lane >= steps) & (lane < 256), 0.0, blocks[later])
    j2 = solved[2][:, :steps]
    j1 = solved[1][:, :steps] - exact(solved[1][:, 256 + 2 * R : 256 + 3 * R], j2)
    j0 = (
        solved[0][:, :steps]
        - exact(solved[0][:, 256 + 2 * R : 256 + 3 * R], j2)
        - exact(solved[0][:, 256 + R : 256 + 2 * R], j1)
    )
    turned = exact(chosen[...], jnp.concatenate([j0, j1, j2], axis=0)).T
    high = turned.astype(jnp.bfloat16)
    weights[:steps] = high
    weights[steps:] = (turned - high.astype(jnp.float32)).astype(jnp.bfloat16)
    load.wait()
    stores = []
    for c in range(points // WIDTH):
        cols = slice(c * WIDTH, (c + 1) * WIDTH)
        slow = jnp.dot(weights[...], y[:, cols], preferred_element_type=jnp.float32)
        out[:, cols] = field[:, cols] - (slow[:steps] + slow[steps:])
        store = pltpu.make_async_copy(out.at[:, cols], out_hbm.at[:, cols], store_sem.at[c])
        store.start()
        stores.append(store)
    for store in stores:
        store.wait()


def body(nt, ns, record, mode_basis, slow_picks, phases):
    steps, points = record.shape
    segs = points // SEG
    owners = max(o for o in (1, 2, 4, 6, 12) if o <= ns)
    group = nt // 4
    dma = pltpu.SemaphoreType.DMA
    vmem = pl.BlockSpec(memory_space=pltpu.VMEM)
    hbm = pl.BlockSpec(memory_space=pl.ANY)
    y, sums, chosen = pl.pallas_call(
        functools.partial(collect, nt, ns, owners),
        out_shape=[
            jax.ShapeDtypeStruct((4 * M, points), jnp.bfloat16),
            jax.ShapeDtypeStruct((LEVELS * R, 384), jnp.float32),
            jax.ShapeDtypeStruct((4 * M, LEVELS * R), jnp.float32),
        ],
        in_specs=[pl.BlockSpec(memory_space=pltpu.SMEM), vmem, hbm, hbm],
        out_specs=[vmem, vmem, vmem],
        scratch_shapes=[
            pltpu.VMEM((segs * steps, SEG), jnp.float32),
            pltpu.VMEM((2 * steps, points), jnp.bfloat16),
            pltpu.VMEM((4 * M, points), jnp.bfloat16),
            pltpu.VMEM(((M // nt + M // group) * segs, SEG), jnp.bfloat16),
            pltpu.VMEM((nt, M // nt * segs, SEG), jnp.bfloat16),
            pltpu.VMEM((group, M // group * segs, SEG), jnp.bfloat16),
            pltpu.VMEM((M * segs, SEG), jnp.float32),
            pltpu.VMEM((LEVELS, M, M), jnp.float32),
            pltpu.VMEM((4 * M, LEVELS * R), jnp.float32),
            pltpu.VMEM((4 * M, steps), jnp.float32),
            pltpu.VMEM((4 * M, 4 * M), jnp.float32),
            pltpu.VMEM((LEVELS * R, 384), jnp.float32),
            pltpu.VMEM((ns, LEVELS * R // owners, 384), jnp.float32),
            pltpu.VMEM((LEVELS * R, 384), jnp.float32),
            dma((segs,)), dma((LEVELS,)),
            dma((nt,)), dma((nt,)), dma((group,)), dma((group,)),
            dma((ns,)), dma((ns,)), dma((ns,)), dma((ns,)),
        ],
        compiler_params=pltpu.CompilerParams(
            collective_id=0, has_side_effects=True, vmem_limit_bytes=VMEM_LIMIT
        ),
        name="collect",
    )(phases, slow_picks, mode_basis, record)
    return pl.pallas_call(
        functools.partial(update, float(points * ns)),
        out_shape=jax.ShapeDtypeStruct((steps, points), jnp.float32),
        in_specs=[vmem, vmem, vmem, hbm],
        out_specs=hbm,
        scratch_shapes=[
            pltpu.VMEM((steps, points), jnp.float32),
            pltpu.VMEM((steps, points), jnp.float32),
            pltpu.VMEM((2 * steps, 4 * M), jnp.bfloat16),
            dma(()), dma((points // WIDTH,)),
        ],
        compiler_params=pltpu.CompilerParams(vmem_limit_bytes=VMEM_LIMIT),
        name="update",
    )(sums, chosen, y, record)


def solution(mesh):
    in_specs = (P("tm", "space"), P(), P(), P())
    out_specs = P("tm", "space")
    return jax.shard_map(
        functools.partial(body, mesh.shape["tm"], mesh.shape["space"]),
        mesh=mesh, in_specs=in_specs, out_specs=out_specs, check_vma=False,
    )
```

time: 559 us -> 56.7 us (0.10)
  blocking collectives: 364 us -> 0 us
  waiting for transfers between devices: 74.3 us -> 0 us
  Pallas kernels: 0 us -> 56.5 us
  other arithmetic: 42.5 us -> 0 us
  matrix products: 37.1 us -> 0 us
  between operations: 18.3 us -> 0.01 us
  local copies, waits for them, and re-layouts: 17.4 us -> 0 us
    psum x6 -> x0, blocking collectives: 321 us -> none  [the longest x3 162 us: local_level(): gram_total = lax.psum(gram_part, 'space')]
    all_gather x1 -> x0, waiting for transfers between devices: 74.3 us -> none  [body(): gathered = lax.all_gather(sampled[0], 'tm', axis=0, tiled=True)]
    pallas_call x0 -> x2, Pallas kernels: none -> 56.5 us  [the longest x1 42.8 us: body(): pl.pallas_call(functools.partial(collect, nt, ns, owners), out_shape=[jax...]
    all_gather x1 -> x0, blocking collectives: 43 us -> none  [body(): gathered = lax.all_gather(sampled[0], 'tm', axis=0, tiled=True)]
    dot_general x21 -> x0, matrix products: 35 us -> none  [the longest x3 15.4 us: remove_slow(): jnp.einsum('wrt,wrp->wtp', amplitude, modes, precision=precise)]
    another operation x15 -> x0, other arithmetic: 29.3 us -> none  [the longest x9 14.9 us: choose_columns(): factor = jnp.linalg.cholesky(kernel)]
    reduce_sum x5 -> x0, other arithmetic: 10 us -> none  [the longest x3 7.96 us: body(): jnp.sum(shaped * select[:, None, :, None], axis=2).astype(jnp.bfloat16)]
    unnamed x16 -> x0, local copies, waits for them, and re-layouts: 7.31 us -> none
  transfers between devices with their start and end apart: 1 -> 0, of which waited for: 1 -> 0; matrix products, arithmetic and copies ran while one was open for 1% -> 0% of each run, Pallas kernels for 0% -> 0%
where the time goes in v1:
time: 56.7 us; the launch traced here: 56.5 us
  Pallas kernels  56.5 us (100%)
    pallas_call x1, Pallas kernels, body(): pl.pallas_call(functools.partial(collect, nt, ns, owners), out_shape=[jax...  42.8 us
    pallas_call x1, Pallas kernels, body(): pl.pallas_call(functools.partial(update, float(points * ns)), out_shape=j...  13.7 us

profile of v1, /device:TPU:1, one launch (start us, length us, event | category | flops | bytes accessed | tf_op | source)
XLA Modules:
  0.0 56.5 jit_solution(7738217553860495770)
XLA Ops:
  0.0 42.8 %collect.1 = (bf16[192,4096]{1,0:T(8,128)(2,1)}, f32[96,384]{1,0:T(8,128)}, f32[192,96]{1,0:T(8,128)}) custom-call(s32[21]{0:T(128)} %phases.1, s32[21,32]{1,0:T(8,128)} %picks.1, f32[21,48,48]{2,1,0:T(8,128)} %basis_hbm.1, f32[192,4096]{1,0:T(8,128)} %record.3), custom_call_target="tpu_custom_call" | custom-call | tf_op jit(solution)/shard_map/collect/pallas_call | solution.py:306
  42.8 13.7 %update.1 = f32[192,4096]{1,0:T(8,128)} custom-call(f32[96,384]{1,0:T(8,128)} %get-tuple-element.8.sums, f32[192,96]{1,0:T(8,128)} %get-tuple-element.9.chosen, bf16[192,4096]{1,0:T(8,128)(2,1)} %get-tuple-element.10.y, f32[192,4096]{1,0:T(8,128)} %record.3), custom_call_target="tpu_custom_call" | custom-call | tf_op jit(solution)/shard_map/update/pallas_call | solution.py:339

commit v2 on v0

v2 whole, which is shorter than its diff:
```python
import jax
import jax.numpy as jnp
from jax import lax
from jax.experimental import pallas as pl
from jax.experimental.pallas import tpu as pltpu
from jax.sharding import PartitionSpec as P

M = 48
R = 32
LANES = 128
WIDTH = 512
EPS = 1e-5
AHEAD = 2
MESH = pl.DeviceIdType.MESH
EXACT = lax.Precision.HIGHEST
VMEM_LIMIT = 24 * 1024 * 1024
NT = 16
NS = 16
NZ = NT // 2
GROUP = 4
STEPS = 192
POINTS = 4096
SEGS = POINTS // LANES
TILES = STEPS // 8
BLOCK = SEGS * 8
ROWS0 = M // NT
ROWS1 = M // GROUP
X0 = STEPS
X1 = X0 + M
X2 = X1 + M
ALL = X2 + 2 * M
LANE1 = 64
LANE0 = 96
OWNERS2 = 8


def dot_nt(a, b):
    return lax.dot_general(a, b, (((1,), (1,)), ((), ())), preferred_element_type=jnp.float32)


def exact(a, b, dims=((1,), (0,))):
    return lax.dot_general(a, b, (dims, ((), ())), precision=EXACT, preferred_element_type=jnp.float32)


def collect(
    phases_hbm, picks_hbm, basis_hbm, record,
    rows, sums, chosen, among,
    phases, picks, field_even, field_odd, got0, got1, wide0, wide1, basis, turned, pad,
    part2, inbox2, total2, part01, inbox01, total01,
    load_sem, small_sem, recv0_sem, sem,
):
    send0_sem, sendy_sem, recvy_sem, send1_sem, recv1_sem = [sem.at[i] for i in range(5)]
    sems2, sems01 = [[sem.at[i] for i in range(j, j + 4)] for j in (5, 9)]
    me_t = lax.axis_index("tm")
    me_s = lax.axis_index("space")
    first = me_t // GROUP * GROUP

    barrier = pltpu.get_barrier_semaphore()
    for d in range(1, NT):
        pl.semaphore_signal(barrier, inc=1, device_id={"tm": lax.rem(me_t + d, NT)}, device_id_type=MESH)
    for d in range(1, NS):
        pl.semaphore_signal(barrier, inc=1, device_id={"space": lax.rem(me_s + d, NS)}, device_id_type=MESH)

    get_phases = pltpu.make_async_copy(phases_hbm, phases, small_sem.at[3])
    get_phases.start()
    load_even, load_odd = [
        pltpu.make_async_copy(record.at[:, i], half.reshape(TILES // 2, BLOCK, LANES), load_sem.at[i])
        for i, half in enumerate((field_even, field_odd))
    ]
    load_even.start()
    q1 = 1 + me_t // GROUP
    q2 = 5 + me_t
    fetches = [
        pltpu.make_async_copy(basis_hbm.at[q], basis.at[level], small_sem.at[level])
        for level, q in enumerate((0, q1, q2))
    ]
    fetches.append(pltpu.make_async_copy(picks_hbm, picks, small_sem.at[4]))
    for fetch in fetches:
        fetch.start()
    load_odd.start()

    get_phases.wait()
    off0 = lax.rem(phases[0], STEPS * NT // M)
    off1 = lax.rem(phases[q1], STEPS * GROUP // M)
    off2 = lax.rem(phases[q2], STEPS // M)
    load_even.wait()
    for r in range(ROWS0):
        start = r * (STEPS // ROWS0) // 16 * BLOCK
        got0[me_t, r * SEGS : (r + 1) * SEGS] = field_even[pl.ds(start + off0, SEGS, stride=8), :].astype(
            jnp.bfloat16
        )
    for r in range(ROWS1):
        start = r * (STEPS // ROWS1) // 16 * BLOCK
        got1[me_t - first, r * SEGS : (r + 1) * SEGS] = field_even[
            pl.ds(start + off1, SEGS, stride=8), :
        ].astype(jnp.bfloat16)

    pl.semaphore_wait(barrier, NT - 1 + NS - 1)

    z = me_t // 2
    h = lax.rem(me_t, 2)
    partner = me_t + 1 - 2 * h
    near = me_t + 2 - 4 * lax.rem(z, 2)
    across = near + 1 - 2 * h

    def along0(target, owner, send_sem, recv_sem):
        return pltpu.make_async_remote_copy(
            src_ref=got0.at[owner], dst_ref=got0.at[owner], send_sem=send_sem, recv_sem=recv_sem,
            device_id={"tm": target}, device_id_type=MESH,
        )

    def along1(target, owner):
        return pltpu.make_async_remote_copy(
            src_ref=got1.at[owner - first], dst_ref=got1.at[owner - first],
            send_sem=send1_sem, recv_sem=recv1_sem,
            device_id={"tm": target}, device_id_type=MESH,
        )

    def whole(ref, count, send_sem, recv_sem):
        place = ref.at[pl.ds(0, count)]
        return pltpu.make_async_remote_copy(
            src_ref=place, dst_ref=place, send_sem=send_sem, recv_sem=recv_sem,
            device_id={"tm": partner}, device_id_type=MESH,
        )

    hops = (1, -1, 2, -2, 3, -3, 4)
    turn = [lax.rem(z + d + NZ, NZ) for d in hops]
    out0 = [along0(2 * turn[i] + h, me_t, send0_sem, recv0_sem.at[z]) for i in range(7)]
    in0 = [along0(2 * turn[i] + h, 2 * turn[i] + h, send0_sem, recv0_sem.at[turn[i]]) for i in range(7)]
    over0 = [along0(partner, 2 * turn[i] + h, sendy_sem, recvy_sem) for i in range(7)]
    over0.append(along0(partner, me_t, sendy_sem, recvy_sem))
    peers1 = (near, partner, across)
    out1 = [along1(peer, me_t) for peer in peers1]
    for copy in (over0[7], *out0, *out1):
        copy.start()

    def widen(wide, got, slot):
        size = got.shape[1]
        wide[pl.ds(pl.multiple_of(slot * size, size), size)] = got[slot].astype(jnp.float32)

    def pass0(i):
        in0[i].wait_recv()
        over0[i].start()
        widen(wide0, got0, 2 * turn[i] + h)

    load_odd.wait()

    def part_columns(c, carry):
        cols = pl.ds(pl.multiple_of(c * LANES, LANES), LANES)
        at = pl.multiple_of(c * 8, 8)
        for p in range(TILES // 2):
            pair = jnp.concatenate(
                [field_even[pl.ds(p * BLOCK + at, 8), :], field_odd[pl.ds(p * BLOCK + at, 8), :]], axis=0
            )
            rows[16 * p : 16 * (p + 1), cols] = pair.astype(jnp.bfloat16)
        x2 = jnp.concatenate(
            [
                half[pl.ds(at + off2 + more, TILES // 2, stride=BLOCK), :]
                for half in (field_even, field_odd)
                for more in (0, 4)
            ],
            axis=0,
        )
        high2 = x2.astype(jnp.bfloat16)
        rows[X2 : X2 + M, cols] = high2
        rows[X2 + M :, cols] = (x2 - high2.astype(jnp.float32)).astype(jnp.bfloat16)
        return carry

    lax.fori_loop(0, SEGS // 2, part_columns, 0)
    widen(wide0, got0, me_t)
    widen(wide1, got1, me_t - first)
    pass0(0)
    pass0(1)
    lax.fori_loop(SEGS // 2, SEGS, part_columns, 0)
    pass0(2)
    pass0(3)

    for fetch in fetches:
        fetch.wait()
    none = lambda count: [jnp.full((1, R), -1, jnp.int32)] * count
    row_m = lax.broadcasted_iota(jnp.int32, (M, LANES), 0)
    for level, (q, place, at) in enumerate(((0, 3, 0), (q1, 2, M), (q2, 0, 2 * M))):
        spots = jnp.concatenate([*none(place), picks[pl.ds(q, 1), :], *none(3 - place)], axis=1)
        columns = exact(basis[level], (row_m == spots).astype(jnp.float32))
        if level == 2:
            pad[...] = columns
            columns = jnp.concatenate([pad[pl.ds(i, M // 4, stride=4), :] for i in range(4)], axis=0)
            chosen[3 * M :] = columns
        chosen[at : at + M] = columns
    turned[...] = chosen[...].T
    at_row = lax.broadcasted_iota(jnp.int32, (STEPS, M), 0)
    order = lax.broadcasted_iota(jnp.int32, (STEPS, M), 1)
    rank = lax.rem(order, M // 4) * 4 + order // (M // 4)
    among[...] = exact((at_row == 4 * rank + off2).astype(jnp.float32), chosen[2 * M : 3 * M])
    for i in range(4, 7):
        pass0(i)

    def put(ref, tiles):
        for g in range(tiles[0].shape[0] // 8):
            for t in range(2):
                ref[2 * g + t] = tiles[t][8 * g : 8 * (g + 1)]

    space = jnp.zeros((R, 2 * LANES - STEPS), jnp.float32)
    by_field2 = exact(turned[:R, 2 * M :], dot_nt(rows[:STEPS], rows[X2:]), ((1,), (1,)))
    put(part2, [by_field2[:, :LANES], jnp.concatenate([by_field2[:, LANES:], space], axis=1)])

    def others(owners, do):
        if owners == NS:
            do(NS - 1)
        else:
            pl.when(me_s < owners)(lambda: do(owners - 1))
            pl.when(me_s >= owners)(lambda: do(owners))

    def spread(part, inbox, sems, owners):
        for d in range(1, NS):
            tgt = lax.rem(me_s + d, NS)
            copy = pltpu.make_async_remote_copy(
                src_ref=part.at[lax.rem(tgt, owners)], dst_ref=inbox.at[me_s],
                send_sem=sems[0], recv_sem=sems[1],
                device_id={"space": tgt}, device_id_type=MESH,
            )
            if owners == NS:
                copy.start()
            else:
                pl.when(tgt < owners)(copy.start)

    def reduce(part, inbox, total, sems, owners):
        def act():
            mine = lax.rem(me_s, owners)
            whole(inbox, NS - 1, sems[0], sems[1]).wait_recv()
            acc = part[mine]
            for d in range(1, NS):
                acc = acc + inbox[lax.rem(me_s + d, NS)]
            total[mine] = acc
            for d in range(1, NS):
                pltpu.make_async_remote_copy(
                    src_ref=total.at[mine], dst_ref=total.at[mine],
                    send_sem=sems[2], recv_sem=sems[3],
                    device_id={"space": lax.rem(me_s + d, NS)}, device_id_type=MESH,
                ).start()

        if owners == NS:
            act()
        else:
            pl.when(me_s < owners)(act)

    def take(total, sems, owners):
        others(owners, lambda count: whole(total, count, sems[2], sems[3]).wait_recv())

    def settle(inbox, sems, owners):
        others(owners, lambda count: whole(inbox, count, sems[0], sems[1]).wait_send())
        finish = whole(inbox, NS - 1, sems[2], sems[3]).wait_send
        if owners == NS:
            finish()
        else:
            pl.when(me_s < owners)(finish)

    spread(part2, inbox2, sems2, OWNERS2)

    def unpack(wide, at):
        for j in range(SEGS):
            rows[at : at + M, j * LANES : (j + 1) * LANES] = wide[pl.ds(j, M, stride=SEGS), :].astype(jnp.bfloat16)

    whole(got1, GROUP - 1, send1_sem, recv1_sem).wait_recv()
    for peer in peers1:
        widen(wide1, got1, peer - first)
    unpack(wide1, X1)
    whole(got0, NZ, sendy_sem, recvy_sem).wait_recv()
    for zz in (*turn, z):
        widen(wide0, got0, 2 * zz + 1 - h)
    unpack(wide0, X0)

    both = dot_nt(rows[:X2], rows[X0:X2])
    mine = turned[LANE1:, : 2 * M]
    by_field = exact(mine, both[:STEPS], ((1,), (1,)))
    by_modes = exact(exact(mine, both[STEPS:], ((1,), (1,))), chosen[: 2 * M])
    put(
        part01,
        [by_field[:, :LANES], jnp.concatenate([by_field[:, LANES:], by_modes[:, LANE1:]], axis=1)],
    )
    spread(part01, inbox01, sems01, NS)
    reduce(part2, inbox2, total2, sems2, OWNERS2)
    reduce(part01, inbox01, total01, sems01, NS)
    take(total2, sems2, OWNERS2)
    sums[16:] = total2[...]
    take(total01, sems01, NS)
    sums[:16] = total01[...]

    whole(got0, NZ - 1, send0_sem, recv0_sem.at[z]).wait_send()
    whole(got0, NZ, sendy_sem, recvy_sem).wait_send()
    whole(got1, GROUP - 1, send1_sem, recv1_sem).wait_send()
    settle(inbox2, sems2, OWNERS2)
    settle(inbox01, sems01, NS)


def eliminate(tiles, pivot_tile, pivot_lane):
    sub = lax.broadcasted_iota(jnp.int32, (8, LANES), 0)
    over = lambda x, i: jnp.broadcast_to(x[i : i + 1], (8, LANES))
    count = len(tiles[0])
    ahead = {}
    for k in range(0, R, 2):
        g, i = divmod(k, 8)
        for j in range(k, min(k + 2 * AHEAD + 2, R)):
            if j not in ahead:
                lane = pivot_lane + j
                ahead[j] = [jnp.broadcast_to(row[pivot_tile][:, lane : lane + 1], (8, LANES)) for row in tiles]
        left, right = ahead.pop(k), ahead.pop(k + 1)
        a, b, c, d = over(left[g], i), over(right[g], i), over(left[g], i + 1), over(right[g], i + 1)
        scale = 1.0 / (a * d - b * c)
        a, b, c, d = a * scale, b * scale, c * scale, d * scale

        def pivot(old):
            first, second = over(old[g], i), over(old[g], i + 1)
            upper, lower = d * first - b * second, a * second - c * first
            moved = [old[q] - (left[q] * upper + right[q] * lower) for q in range(len(old))]
            moved[g] = jnp.where(sub == i, upper, jnp.where(sub == i + 1, lower, moved[g]))
            return moved

        ahead = {j: pivot(old) for j, old in ahead.items()}
        columns = [pivot([row[t] for row in tiles]) for t in range(count)]
        tiles = [[columns[t][q] for t in range(count)] for q in range(R // 8)]
    return tiles


def solve(block, pivot):
    tile, at = divmod(pivot, LANES)
    sub = lax.broadcasted_iota(jnp.int32, (8, LANES), 0)
    lane = lax.broadcasted_iota(jnp.int32, (8, LANES), 1)
    tiles = [
        [block[8 * g : 8 * (g + 1), LANES * t : LANES * (t + 1)] for t in range(block.shape[1] // LANES)]
        for g in range(R // 8)
    ]
    for g in range(R // 8):
        tiles[g][tile] = jnp.where(lane == at + 8 * g + sub, tiles[g][tile] + EPS, tiles[g][tile])
    done = eliminate(tiles, tile, at)
    return jnp.concatenate([jnp.concatenate(row, axis=1) for row in done], axis=0)


def update(sums, chosen, among, rows, record, out_hbm, field, out, weights, load_sem, store_sem):
    load = pltpu.make_async_copy(record, field, load_sem)
    load.start()
    scale = 1.0 / (POINTS * NS)
    tall = lambda first, t: jnp.concatenate([sums[first + 2 * g + t] for g in range(R // 8)], axis=0) * scale
    blocks = []
    for first in (8, 0, 16):
        left, right = tall(first, 0), tall(first, 1)
        by_field = jnp.concatenate([left, right], axis=1)[:, :STEPS]
        blocks.append(jnp.concatenate([left, right, exact(by_field, among[...])], axis=1))
    at1, at0, at2 = LANES + LANE1, LANES + LANE0, 2 * LANES

    def change(level, done, at):
        cols = slice(at, at + R)
        return exact(blocks[level][:, cols] + EPS * done[:, cols], done, ((0,), (0,)))

    done0 = solve(blocks[0], at0)
    blocks[1] = blocks[1] - change(0, done0, at1)
    blocks[2] = blocks[2] - change(0, done0, at2)
    done1 = solve(blocks[1], at1)
    blocks[2] = blocks[2] - change(1, done1, at2)
    pick0 = chosen[:M, LANE0 : LANE0 + R]
    pick1 = chosen[M : 2 * M, LANE1 : LANE1 + R]
    pick2 = chosen[2 * M :, :R]
    way0 = pick0
    way1 = -exact(pick0, done0[:, at1 : at1 + R])
    way2 = -exact(pick0, done0[:, at2 : at2 + R]) - exact(way1, done1[:, at2 : at2 + R])
    low2 = -exact(pick1, done1[:, at2 : at2 + R])
    part0 = exact(done0[:, :STEPS], way0, ((0,), (1,))) + exact(done1[:, :STEPS], way1, ((0,), (1,)))
    part1 = exact(done1[:, :STEPS], pick1, ((0,), (1,)))
    last = jnp.concatenate([way2, low2, pick2], axis=0)
    early = jnp.concatenate([part0, part1, jnp.zeros((STEPS, 2 * M), jnp.float32)], axis=1)
    done2 = solve(blocks[2], at2)
    slopes = early + exact(done2[:, :STEPS], last, ((0,), (1,)))
    high = slopes.astype(jnp.bfloat16)
    weights[:STEPS] = high
    weights[STEPS:] = (slopes - high.astype(jnp.float32)).astype(jnp.bfloat16)
    load.wait()
    stores = []
    for c in range(POINTS // WIDTH):
        cols = slice(c * WIDTH, (c + 1) * WIDTH)
        slow = jnp.dot(weights[...], rows[X0:, cols], preferred_element_type=jnp.float32)
        out[:, cols] = field[:, cols] - (slow[:STEPS] + slow[STEPS:])
        store = pltpu.make_async_copy(out.at[:, cols], out_hbm.at[:, cols], store_sem.at[c])
        store.start()
        stores.append(store)
    for store in stores:
        store.wait()


def body(record, mode_basis, slow_picks, phases):
    dma = pltpu.SemaphoreType.DMA
    vmem = pl.BlockSpec(memory_space=pltpu.VMEM)
    hbm = pl.BlockSpec(memory_space=pltpu.MemorySpace.HBM)
    tiled = record.reshape(TILES, 8, SEGS, LANES).transpose(0, 2, 1, 3).reshape(TILES // 2, 2, BLOCK, LANES)
    far = lambda x: pltpu.with_memory_space_constraint(x, pltpu.MemorySpace.HBM)
    chunk = lambda count: pltpu.VMEM((count, 8, LANES), jnp.float32)
    rows, sums, chosen, among = pl.pallas_call(
        collect,
        out_shape=[
            pltpu.VMEM((ALL, POINTS), jnp.bfloat16),
            pltpu.VMEM((24, 8, LANES), jnp.float32),
            pltpu.VMEM((4 * M, LANES), jnp.float32),
            pltpu.VMEM((STEPS, LANES), jnp.float32),
        ],
        in_specs=[hbm] * 4,
        out_specs=[vmem] * 4,
        scratch_shapes=[
            pltpu.SMEM((21,), jnp.int32),
            pltpu.VMEM((21, R), jnp.int32),
            pltpu.VMEM((TILES // 2 * BLOCK, LANES), jnp.float32),
            pltpu.VMEM((TILES // 2 * BLOCK, LANES), jnp.float32),
            pltpu.VMEM((NT, ROWS0 * SEGS, LANES), jnp.bfloat16),
            pltpu.VMEM((GROUP, ROWS1 * SEGS, LANES), jnp.bfloat16),
            pltpu.VMEM((M * SEGS, LANES), jnp.float32),
            pltpu.VMEM((M * SEGS, LANES), jnp.float32),
            pltpu.VMEM((3, M, M), jnp.float32),
            pltpu.VMEM((LANES, 4 * M), jnp.float32),
            pltpu.VMEM((M, LANES), jnp.float32),
            chunk(8), chunk(NS), chunk(8), chunk(16), chunk(NS), chunk(16),
            dma((2,)), dma((5,)), dma((NZ,)), dma((13,)),
        ],
        compiler_params=pltpu.CompilerParams(
            collective_id=0, has_side_effects=True, vmem_limit_bytes=VMEM_LIMIT
        ),
        name="collect",
    )(far(phases), far(slow_picks), far(mode_basis), far(tiled))
    near = lambda x: pltpu.with_memory_space_constraint(x, pltpu.VMEM)
    return pl.pallas_call(
        update,
        out_shape=jax.ShapeDtypeStruct((STEPS, POINTS), jnp.float32),
        in_specs=[vmem, vmem, vmem, vmem, hbm],
        out_specs=hbm,
        scratch_shapes=[
            pltpu.VMEM((STEPS, POINTS), jnp.float32),
            pltpu.VMEM((STEPS, POINTS), jnp.float32),
            pltpu.VMEM((2 * STEPS, 4 * M), jnp.bfloat16),
            dma(()), dma((POINTS // WIDTH,)),
        ],
        compiler_params=pltpu.CompilerParams(vmem_limit_bytes=VMEM_LIMIT),
        name="update",
    )(near(sums), near(chosen), near(among), near(rows), far(record))


def solution(mesh):
    in_specs = (P("tm", "space"), P(), P(), P())
    return jax.shard_map(body, mesh=mesh, in_specs=in_specs, out_specs=P("tm", "space"), check_vma=False)
```

time: 559 us -> 40.3 us (0.07)
  blocking collectives: 364 us -> 0 us
  waiting for transfers between devices: 74.3 us -> 0 us
  other arithmetic: 42.5 us -> 0 us
  Pallas kernels: 0 us -> 40.2 us
  matrix products: 37.1 us -> 0 us
  between operations: 18.3 us -> 0.01 us
  local copies, waits for them, and re-layouts: 17.4 us -> 0 us
    psum x6 -> x0, blocking collectives: 321 us -> none  [the longest x3 162 us: local_level(): gram_total = lax.psum(gram_part, 'space')]
    all_gather x1 -> x0, waiting for transfers between devices: 74.3 us -> none  [body(): gathered = lax.all_gather(sampled[0], 'tm', axis=0, tiled=True)]
    all_gather x1 -> x0, blocking collectives: 43 us -> none  [body(): gathered = lax.all_gather(sampled[0], 'tm', axis=0, tiled=True)]
    pallas_call x0 -> x2, Pallas kernels: none -> 40.2 us  [the longest x1 32.5 us: body(): pl.pallas_call(collect, out_shape=[pltpu.VMEM((ALL, POINTS), jnp.bfloat16...]
    dot_general x21 -> x0, matrix products: 35 us -> none  [the longest x3 15.4 us: remove_slow(): jnp.einsum('wrt,wrp->wtp', amplitude, modes, precision=precise)]
    another operation x15 -> x0, other arithmetic: 29.3 us -> none  [the longest x9 14.9 us: choose_columns(): factor = jnp.linalg.cholesky(kernel)]
    reduce_sum x5 -> x0, other arithmetic: 10 us -> none  [the longest x3 7.96 us: body(): jnp.sum(shaped * select[:, None, :, None], axis=2).astype(jnp.bfloat16)]
    unnamed x16 -> x0, local copies, waits for them, and re-layouts: 7.31 us -> none
  transfers between devices with their start and end apart: 1 -> 0, of which waited for: 1 -> 0; matrix products, arithmetic and copies ran while one was open for 1% -> 0% of each run, Pallas kernels for 0% -> 0%
where the time goes in v2:
time: 40.3 us; the launch traced here: 40.2 us
  Pallas kernels  40.2 us (100%)
    pallas_call x1, Pallas kernels, body(): pl.pallas_call(collect, out_shape=[pltpu.VMEM((ALL, POINTS), jnp.bfloat16...  32.5 us
    pallas_call x1, Pallas kernels, body(): pl.pallas_call(update, out_shape=jax.ShapeDtypeStruct((STEPS, POINTS), jn...  7.74 us

profile of v2, /device:TPU:1, one launch (start us, length us, event | category | flops | bytes accessed | tf_op | source)
XLA Modules:
  0.0 40.2 jit_solution(4491967135626666832)
XLA Ops:
  0.0 32.5 %collect.1 = (bf16[384,4096]{1,0:T(8,128)(2,1)S(1)}, f32[24,8,128]{2,1,0:T(8,128)S(1)}, f32[192,128]{1,0:T(8,128)S(1)}, f32[192,128]{1,0:T(8,128)S(1)}) custom-call(s32[21]{0:T(128)} %phases_hbm.1, s32[21,32]{1,0:T(8,128)} %picks_hbm.1, f32[21,48,48]{2,1,0:T(8,128)} %basis_hbm.1, f32[12,2,256,128]{3,2,1,0:T(8,128)} %bitcast.5), custom_call_target="tpu_custom_call" | custom-call | tf_op jit(solution)/shard_map/collect/pallas_call | solution.py:396
  32.5 7.7 %update.1 = f32[192,4096]{1,0:T(8,128)} custom-call(f32[24,8,128]{2,1,0:T(8,128)S(1)} %get-tuple-element.9.sums, f32[192,128]{1,0:T(8,128)S(1)} %get-tuple-element.10.chosen, f32[192,128]{1,0:T(8,128)S(1)} %get-tuple-element.11.among, bf16[384,4096]{1,0:T(8,128)(2,1)S(1)} %get-tuple-element.12.rows, f32[192,4096]{1,0:T(8,128)} %record.1), custom_call_target="tpu_custom_call" | custom-call | tf_op jit(solution)/shard_map/update/pallas_call | solution.py:427

commit v3 on v2

--- a/solution.py
+++ b/solution.py
@@ -10,13 +10,14 @@
 LANES = 128
 WIDTH = 512
 EPS = 1e-5
-AHEAD = 2
+AHEAD = 4
 MESH = pl.DeviceIdType.MESH
 EXACT = lax.Precision.HIGHEST
 VMEM_LIMIT = 24 * 1024 * 1024
 NT = 16
 NS = 16
 NZ = NT // 2
+CHIPS = NS // 2
 GROUP = 4
 STEPS = 192
 POINTS = 4096
@@ -45,12 +46,14 @@
 def collect(
     phases_hbm, picks_hbm, basis_hbm, record,
     rows, sums, chosen, among,
-    phases, picks, field_even, field_odd, got0, got1, wide0, wide1, basis, turned, pad,
-    part2, inbox2, total2, part01, inbox01, total01,
+    phases, picks, head, field_even, field_odd, got0, got1, wide0, wide1, basis, turned, pad,
+    part2, inbox2, total2, part01, inbox_mate, halves, total01,
     load_sem, small_sem, recv0_sem, sem,
 ):
     send0_sem, sendy_sem, recvy_sem, send1_sem, recv1_sem = [sem.at[i] for i in range(5)]
-    sems2, sems01 = [[sem.at[i] for i in range(j, j + 4)] for j in (5, 9)]
+    recvp_sem = sem.at[15]
+    sems2 = [sem.at[i] for i in range(5, 9)]
+    mate_sems, chip_sems, back_sems = [[sem.at[j], sem.at[j + 1]] for j in (9, 11, 13)]
     me_t = lax.axis_index("tm")
     me_s = lax.axis_index("space")
     first = me_t // GROUP * GROUP
@@ -64,9 +67,11 @@
     get_phases = pltpu.make_async_copy(phases_hbm, phases, small_sem.at[3])
     get_phases.start()
     load_even, load_odd = [
-        pltpu.make_async_copy(record.at[:, i], half.reshape(TILES // 2, BLOCK, LANES), load_sem.at[i])
+        pltpu.make_async_copy(record.at[:, :, i], half.reshape(ROWS0, ROWS1 // ROWS0, BLOCK, LANES), load_sem.at[i])
         for i, half in enumerate((field_even, field_odd))
     ]
+    load_head = pltpu.make_async_copy(record.at[:, 0, 0], head.reshape(ROWS0, BLOCK, LANES), load_sem.at[2])
+    load_head.start()
     load_even.start()
     q1 = 1 + me_t // GROUP
     q2 = 5 + me_t
@@ -83,17 +88,9 @@
     off0 = lax.rem(phases[0], STEPS * NT // M)
     off1 = lax.rem(phases[q1], STEPS * GROUP // M)
     off2 = lax.rem(phases[q2], STEPS // M)
-    load_even.wait()
+    load_head.wait()
     for r in range(ROWS0):
-        start = r * (STEPS // ROWS0) // 16 * BLOCK
-        got0[me_t, r * SEGS : (r + 1) * SEGS] = field_even[pl.ds(start + off0, SEGS, stride=8), :].astype(
-            jnp.bfloat16
-        )
-    for r in range(ROWS1):
-        start = r * (STEPS // ROWS1) // 16 * BLOCK
-        got1[me_t - first, r * SEGS : (r + 1) * SEGS] = field_even[
-            pl.ds(start + off1, SEGS, stride=8), :
-        ].astype(jnp.bfloat16)
+        got0[me_t, r * SEGS : (r + 1) * SEGS] = head[pl.ds(r * BLOCK + off0, SEGS, stride=8), :].astype(jnp.bfloat16)
 
     pl.semaphore_wait(barrier, NT - 1 + NS - 1)
 
@@ -109,10 +106,10 @@
             device_id={"tm": target}, device_id_type=MESH,
         )
 
-    def along1(target, owner):
+    def along1(target, owner, recv_sem):
         return pltpu.make_async_remote_copy(
             src_ref=got1.at[owner - first], dst_ref=got1.at[owner - first],
-            send_sem=send1_sem, recv_sem=recv1_sem,
+            send_sem=send1_sem, recv_sem=recv_sem,
             device_id={"tm": target}, device_id_type=MESH,
         )
 
@@ -130,13 +127,22 @@
     over0 = [along0(partner, 2 * turn[i] + h, sendy_sem, recvy_sem) for i in range(7)]
     over0.append(along0(partner, me_t, sendy_sem, recvy_sem))
     peers1 = (near, partner, across)
-    out1 = [along1(peer, me_t) for peer in peers1]
-    for copy in (over0[7], *out0, *out1):
+    out1 = [along1(near, me_t, recv1_sem), along1(partner, me_t, recvp_sem), along1(near, partner, recv1_sem)]
+    in_partner = along1(partner, partner, recvp_sem)
+    for copy in (over0[7], *out0):
         copy.start()
+    load_even.wait()
+    for r in range(ROWS1):
+        got1[me_t - first, r * SEGS : (r + 1) * SEGS] = field_even[
+            pl.ds(r * BLOCK + off1, SEGS, stride=8), :
+        ].astype(jnp.bfloat16)
+    for copy in (out1[1], out1[0]):
+        copy.start()
 
     def widen(wide, got, slot):
-        size = got.shape[1]
-        wide[pl.ds(pl.multiple_of(slot * size, size), size)] = got[slot].astype(jnp.float32)
+        count = got.shape[1] // SEGS
+        for r in range(count):
+            wide[pl.ds(slot * count + r, SEGS, stride=M), :] = got[slot, r * SEGS : (r + 1) * SEGS].astype(jnp.float32)
 
     def pass0(i):
         in0[i].wait_recv()
@@ -166,14 +172,9 @@
         rows[X2 + M :, cols] = (x2 - high2.astype(jnp.float32)).astype(jnp.bfloat16)
         return carry
 
-    lax.fori_loop(0, SEGS // 2, part_columns, 0)
+    lax.fori_loop(0, SEGS, part_columns, 0)
     widen(wide0, got0, me_t)
     widen(wide1, got1, me_t - first)
-    pass0(0)
-    pass0(1)
-    lax.fori_loop(SEGS // 2, SEGS, part_columns, 0)
-    pass0(2)
-    pass0(3)
 
     for fetch in fetches:
         fetch.wait()
@@ -192,9 +193,6 @@
     order = lax.broadcasted_iota(jnp.int32, (STEPS, M), 1)
     rank = lax.rem(order, M // 4) * 4 + order // (M // 4)
     among[...] = exact((at_row == 4 * rank + off2).astype(jnp.float32), chosen[2 * M : 3 * M])
-    for i in range(4, 7):
-        pass0(i)
-
     def put(ref, tiles):
         for g in range(tiles[0].shape[0] // 8):
             for t in range(2):
@@ -204,64 +202,44 @@
     by_field2 = exact(turned[:R, 2 * M :], dot_nt(rows[:STEPS], rows[X2:]), ((1,), (1,)))
     put(part2, [by_field2[:, :LANES], jnp.concatenate([by_field2[:, LANES:], space], axis=1)])
 
-    def others(owners, do):
-        if owners == NS:
-            do(NS - 1)
-        else:
-            pl.when(me_s < owners)(lambda: do(owners - 1))
-            pl.when(me_s >= owners)(lambda: do(owners))
-
-    def spread(part, inbox, sems, owners):
+    def others(do):
+        pl.when(me_s < OWNERS2)(lambda: do(OWNERS2 - 1))
+        pl.when(me_s >= OWNERS2)(lambda: do(OWNERS2))
+
+    for d in range(1, NS):
+        tgt = lax.rem(me_s + d, NS)
+        copy = pltpu.make_async_remote_copy(
+            src_ref=part2.at[lax.rem(tgt, OWNERS2)], dst_ref=inbox2.at[me_s],
+            send_sem=sems2[0], recv_sem=sems2[1],
+            device_id={"space": tgt}, device_id_type=MESH,
+        )
+        pl.when(tgt < OWNERS2)(copy.start)
+
+    for i in range(7):
+        pass0(i)
+        if i == 3:
+            in_partner.wait_recv()
+            out1[2].start()
+
+    @pl.when(me_s < OWNERS2)
+    def _():
+        own = lax.rem(me_s, OWNERS2)
+        whole(inbox2, NS - 1, sems2[0], sems2[1]).wait_recv()
+        acc = part2[own]
         for d in range(1, NS):
-            tgt = lax.rem(me_s + d, NS)
-            copy = pltpu.make_async_remote_copy(
-                src_ref=part.at[lax.rem(tgt, owners)], dst_ref=inbox.at[me_s],
-                send_sem=sems[0], recv_sem=sems[1],
-                device_id={"space": tgt}, device_id_type=MESH,
-            )
-            if owners == NS:
-                copy.start()
-            else:
-                pl.when(tgt < owners)(copy.start)
-
-    def reduce(part, inbox, total, sems, owners):
-        def act():
-            mine = lax.rem(me_s, owners)
-            whole(inbox, NS - 1, sems[0], sems[1]).wait_recv()
-            acc = part[mine]
-            for d in range(1, NS):
-                acc = acc + inbox[lax.rem(me_s + d, NS)]
-            total[mine] = acc
-            for d in range(1, NS):
-                pltpu.make_async_remote_copy(
-                    src_ref=total.at[mine], dst_ref=total.at[mine],
-                    send_sem=sems[2], recv_sem=sems[3],
-                    device_id={"space": lax.rem(me_s + d, NS)}, device_id_type=MESH,
-                ).start()
-
-        if owners == NS:
-            act()
-        else:
-            pl.when(me_s < owners)(act)
-
-    def take(total, sems, owners):
-        others(owners, lambda count: whole(total, count, sems[2], sems[3]).wait_recv())
-
-    def settle(inbox, sems, owners):
-        others(owners, lambda count: whole(inbox, count, sems[0], sems[1]).wait_send())
-        finish = whole(inbox, NS - 1, sems[2], sems[3]).wait_send
-        if owners == NS:
-            finish()
-        else:
-            pl.when(me_s < owners)(finish)
-
-    spread(part2, inbox2, sems2, OWNERS2)
+            acc = acc + inbox2[lax.rem(me_s + d, NS)]
+        total2[own] = acc
+        for d in range(1, NS):
+            pltpu.make_async_remote_copy(
+                src_ref=total2.at[own], dst_ref=total2.at[own], send_sem=sems2[2], recv_sem=sems2[3],
+                device_id={"space": lax.rem(me_s + d, NS)}, device_id_type=MESH,
+            ).start()
 
     def unpack(wide, at):
         for j in range(SEGS):
-            rows[at : at + M, j * LANES : (j + 1) * LANES] = wide[pl.ds(j, M, stride=SEGS), :].astype(jnp.bfloat16)
-
-    whole(got1, GROUP - 1, send1_sem, recv1_sem).wait_recv()
+            rows[at : at + M, j * LANES : (j + 1) * LANES] = wide[j * M : (j + 1) * M].astype(jnp.bfloat16)
+
+    whole(got1, 2, send1_sem, recv1_sem).wait_recv()
     for peer in peers1:
         widen(wide1, got1, peer - first)
     unpack(wide1, X1)
@@ -278,19 +256,47 @@
         part01,
         [by_field[:, :LANES], jnp.concatenate([by_field[:, LANES:], by_modes[:, LANE1:]], axis=1)],
     )
-    spread(part01, inbox01, sems01, NS)
-    reduce(part2, inbox2, total2, sems2, OWNERS2)
-    reduce(part01, inbox01, total01, sems01, NS)
-    take(total2, sems2, OWNERS2)
+
+    core = lax.rem(me_s, 2)
+    chip = me_s // 2
+    mate = me_s + 1 - 2 * core
+    mine = pl.ds(core * 8, 8)
+
+    def to_mate(src, dst, sems):
+        return pltpu.make_async_remote_copy(
+            src_ref=src, dst_ref=dst, send_sem=sems[0], recv_sem=sems[1],
+            device_id={"space": mate}, device_id_type=MESH,
+        )
+
+    give = to_mate(part01.at[pl.ds(8 - core * 8, 8)], inbox_mate, mate_sems)
+    give.start()
+    give.wait_recv()
+    halves[chip] = part01[mine] + inbox_mate[...]
+    for d in range(1, CHIPS):
+        pltpu.make_async_remote_copy(
+            src_ref=halves.at[chip], dst_ref=halves.at[chip], send_sem=chip_sems[0], recv_sem=chip_sems[1],
+            device_id={"space": 2 * lax.rem(chip + d, CHIPS) + core}, device_id_type=MESH,
+        ).start()
+    whole(halves, CHIPS - 1, chip_sems[0], chip_sems[1]).wait_recv()
+    acc = halves[0]
+    for i in range(1, CHIPS):
+        acc = acc + halves[i]
+    total01[mine] = acc
+    back = to_mate(total01.at[mine], total01.at[mine], back_sems)
+    back.start()
+    others(lambda count: whole(total2, count, sems2[2], sems2[3]).wait_recv())
     sums[16:] = total2[...]
-    take(total01, sems01, NS)
+    back.wait_recv()
     sums[:16] = total01[...]
 
     whole(got0, NZ - 1, send0_sem, recv0_sem.at[z]).wait_send()
     whole(got0, NZ, sendy_sem, recvy_sem).wait_send()
     whole(got1, GROUP - 1, send1_sem, recv1_sem).wait_send()
-    settle(inbox2, sems2, OWNERS2)
-    settle(inbox01, sems01, NS)
+    others(lambda count: whole(inbox2, count, sems2[0], sems2[1]).wait_send())
+    pl.when(me_s < OWNERS2)(whole(inbox2, NS - 1, sems2[2], sems2[3]).wait_send)
+    give.wait_send()
+    whole(halves, CHIPS - 1, chip_sems[0], chip_sems[1]).wait_send()
+    back.wait_send()
 
 
 def eliminate(tiles, pivot_tile, pivot_lane):
@@ -336,43 +342,54 @@
     return jnp.concatenate([jnp.concatenate(row, axis=1) for row in done], axis=0)
 
 
-def update(sums, chosen, among, rows, record, out_hbm, field, out, weights, load_sem, store_sem):
+def update(sums, chosen, among, rows, record, out_hbm, field, out, weights, held, load_sem, store_sem):
+    live = lax.axis_index("tm") >= 0
+
     load = pltpu.make_async_copy(record, field, load_sem)
     load.start()
-    scale = 1.0 / (POINTS * NS)
-    tall = lambda first, t: jnp.concatenate([sums[first + 2 * g + t] for g in range(R // 8)], axis=0) * scale
-    blocks = []
-    for first in (8, 0, 16):
-        left, right = tall(first, 0), tall(first, 1)
-        by_field = jnp.concatenate([left, right], axis=1)[:, :STEPS]
-        blocks.append(jnp.concatenate([left, right, exact(by_field, among[...])], axis=1))
-    at1, at0, at2 = LANES + LANE1, LANES + LANE0, 2 * LANES
-
-    def change(level, done, at):
-        cols = slice(at, at + R)
-        return exact(blocks[level][:, cols] + EPS * done[:, cols], done, ((0,), (0,)))
-
-    done0 = solve(blocks[0], at0)
-    blocks[1] = blocks[1] - change(0, done0, at1)
-    blocks[2] = blocks[2] - change(0, done0, at2)
-    done1 = solve(blocks[1], at1)
-    blocks[2] = blocks[2] - change(1, done1, at2)
-    pick0 = chosen[:M, LANE0 : LANE0 + R]
-    pick1 = chosen[M : 2 * M, LANE1 : LANE1 + R]
-    pick2 = chosen[2 * M :, :R]
-    way0 = pick0
-    way1 = -exact(pick0, done0[:, at1 : at1 + R])
-    way2 = -exact(pick0, done0[:, at2 : at2 + R]) - exact(way1, done1[:, at2 : at2 + R])
-    low2 = -exact(pick1, done1[:, at2 : at2 + R])
-    part0 = exact(done0[:, :STEPS], way0, ((0,), (1,))) + exact(done1[:, :STEPS], way1, ((0,), (1,)))
-    part1 = exact(done1[:, :STEPS], pick1, ((0,), (1,)))
-    last = jnp.concatenate([way2, low2, pick2], axis=0)
-    early = jnp.concatenate([part0, part1, jnp.zeros((STEPS, 2 * M), jnp.float32)], axis=1)
-    done2 = solve(blocks[2], at2)
-    slopes = early + exact(done2[:, :STEPS], last, ((0,), (1,)))
-    high = slopes.astype(jnp.bfloat16)
-    weights[:STEPS] = high
-    weights[STEPS:] = (slopes - high.astype(jnp.float32)).astype(jnp.bfloat16)
+    @pl.when(live)
+    def _():
+        scale = 1.0 / (POINTS * NS)
+        tall = lambda first, t: jnp.concatenate([sums[first + 2 * g + t] for g in range(R // 8)], axis=0) * scale
+        blocks = []
+        for first in (8, 0, 16):
+            left, right = tall(first, 0), tall(first, 1)
+            by_field = jnp.concatenate([left, right], axis=1)[:, :STEPS]
+            blocks.append(jnp.concatenate([left, right, exact(by_field, among[...])], axis=1))
+        for level in range(3):
+            held[level] = blocks[level]
+
+    @pl.when(live)
+    def _():
+        blocks = [held[level] for level in range(3)]
+        at1, at0, at2 = LANES + LANE1, LANES + LANE0, 2 * LANES
+
+        def change(level, done, at):
+            cols = slice(at, at + R)
+            return exact(blocks[level][:, cols] + EPS * done[:, cols], done, ((0,), (0,)))
+
+        done0 = solve(blocks[0], at0)
+        blocks[1] = blocks[1] - change(0, done0, at1)
+        blocks[2] = blocks[2] - change(0, done0, at2)
+        done1 = solve(blocks[1], at1)
+        blocks[2] = blocks[2] - change(1, done1, at2)
+        pick0 = chosen[:M, LANE0 : LANE0 + R]
+        pick1 = chosen[M : 2 * M, LANE1 : LANE1 + R]
+        pick2 = chosen[2 * M :, :R]
+        way0 = pick0
+        way1 = -exact(pick0, done0[:, at1 : at1 + R])
+        way2 = -exact(pick0, done0[:, at2 : at2 + R]) - exact(way1, done1[:, at2 : at2 + R])
+        low2 = -exact(pick1, done1[:, at2 : at2 + R])
+        part0 = exact(done0[:, :STEPS], way0, ((0,), (1,))) + exact(done1[:, :STEPS], way1, ((0,), (1,)))
+        part1 = exact(done1[:, :STEPS], pick1, ((0,), (1,)))
+        last = jnp.concatenate([way2, low2, pick2], axis=0)
+        early = jnp.concatenate([part0, part1, jnp.zeros((STEPS, 2 * M), jnp.float32)], axis=1)
+        done2 = solve(blocks[2], at2)
+        slopes = early + exact(done2[:, :STEPS], last, ((0,), (1,)))
+        high = slopes.astype(jnp.bfloat16)
+        weights[:STEPS] = high
+        weights[STEPS:] = (slopes - high.astype(jnp.float32)).astype(jnp.bfloat16)
+
     load.wait()
     stores = []
     for c in range(POINTS // WIDTH):
@@ -390,9 +407,9 @@
     dma = pltpu.SemaphoreType.DMA
     vmem = pl.BlockSpec(memory_space=pltpu.VMEM)
     hbm = pl.BlockSpec(memory_space=pltpu.MemorySpace.HBM)
-    tiled = record.reshape(TILES, 8, SEGS, LANES).transpose(0, 2, 1, 3).reshape(TILES // 2, 2, BLOCK, LANES)
+    tiled = record.reshape(TILES, 8, SEGS, LANES).transpose(0, 2, 1, 3).reshape(ROWS0, ROWS1 // ROWS0, 2, BLOCK, LANES)
     far = lambda x: pltpu.with_memory_space_constraint(x, pltpu.MemorySpace.HBM)
-    chunk = lambda count: pltpu.VMEM((count, 8, LANES), jnp.float32)
+    chunk = lambda *count: pltpu.VMEM((*count, 8, LANES), jnp.float32)
     rows, sums, chosen, among = pl.pallas_call(
         collect,
         out_shape=[
@@ -406,6 +423,7 @@
         scratch_shapes=[
             pltpu.SMEM((21,), jnp.int32),
             pltpu.VMEM((21, R), jnp.int32),
+            pltpu.VMEM((ROWS0 * BLOCK, LANES), jnp.float32),
             pltpu.VMEM((TILES // 2 * BLOCK, LANES), jnp.float32),
             pltpu.VMEM((TILES // 2 * BLOCK, LANES), jnp.float32),
             pltpu.VMEM((NT, ROWS0 * SEGS, LANES), jnp.bfloat16),
@@ -415,8 +433,8 @@
             pltpu.VMEM((3, M, M), jnp.float32),
             pltpu.VMEM((LANES, 4 * M), jnp.float32),
             pltpu.VMEM((M, LANES), jnp.float32),
-            chunk(8), chunk(NS), chunk(8), chunk(16), chunk(NS), chunk(16),
-            dma((2,)), dma((5,)), dma((NZ,)), dma((13,)),
+            chunk(8), chunk(NS), chunk(8), chunk(16), chunk(8), chunk(CHIPS, 8), chunk(16),
+            dma((3,)), dma((5,)), dma((NZ,)), dma((16,)),
         ],
         compiler_params=pltpu.CompilerParams(
             collective_id=0, has_side_effects=True, vmem_limit_bytes=VMEM_LIMIT
@@ -433,6 +451,7 @@
             pltpu.VMEM((STEPS, POINTS), jnp.float32),
             pltpu.VMEM((STEPS, POINTS), jnp.float32),
             pltpu.VMEM((2 * STEPS, 4 * M), jnp.bfloat16),
+            pltpu.VMEM((3, R, 3 * LANES), jnp.float32),
             dma(()), dma((POINTS // WIDTH,)),
         ],
         compiler_params=pltpu.CompilerParams(vmem_limit_bytes=VMEM_LIMIT),

time: 40.3 us -> 37.4 us (0.928)
  Pallas kernels: 40.2 us -> 37.3 us
    pallas_call x1, Pallas kernels: 7.74 us -> 5.81 us  [body(): pl.pallas_call(update, out_shape=jax.ShapeDtypeStruct((STEPS, POINTS), jn...]
    pallas_call x1, Pallas kernels: 32.5 us -> 31.5 us  [body(): pl.pallas_call(collect, out_shape=[pltpu.VMEM((ALL, POINTS), jnp.bfloat16...]
where the time goes in v3:
time: 37.4 us; the launch traced here: 37.3 us
  Pallas kernels  37.3 us (100%)
    pallas_call x1, Pallas kernels, body(): pl.pallas_call(collect, out_shape=[pltpu.VMEM((ALL, POINTS), jnp.bfloat16...  31.5 us
    pallas_call x1, Pallas kernels, body(): pl.pallas_call(update, out_shape=jax.ShapeDtypeStruct((STEPS, POINTS), jn...  5.81 us

profile of v3, /device:TPU:1, one launch (start us, length us, event | category | flops | bytes accessed | tf_op | source)
XLA Modules:
  0.0 37.3 jit_solution(9094322799414454426)
XLA Ops:
  0.0 31.5 %collect.1 = (bf16[384,4096]{1,0:T(8,128)(2,1)S(1)}, f32[24,8,128]{2,1,0:T(8,128)S(1)}, f32[192,128]{1,0:T(8,128)S(1)}, f32[192,128]{1,0:T(8,128)S(1)}) custom-call(s32[21]{0:T(128)} %phases_hbm.1, s32[21,32]{1,0:T(8,128)} %picks_hbm.1, f32[21,48,48]{2,1,0:T(8,128)} %basis_hbm.1, f32[3,4,2,256,128]{4,3,2,1,0:T(8,128)} %bitcast.5), custom_call_target="tpu_custom_call" | custom-call | tf_op jit(solution)/shard_map/collect/pallas_call | solution.py:413
  31.5 5.8 %update.1 = f32[192,4096]{1,0:T(8,128)} custom-call(f32[24,8,128]{2,1,0:T(8,128)S(1)} %get-tuple-element.9.sums, f32[192,128]{1,0:T(8,128)S(1)} %get-tuple-element.10.chosen, f32[192,128]{1,0:T(8,128)S(1)} %get-tuple-element.11.among, bf16[384,4096]{1,0:T(8,128)(2,1)S(1)} %get-tuple-element.12.rows, f32[192,4096]{1,0:T(8,128)} %record.1), custom_call_target="tpu_custom_call" | custom-call | tf_op jit(solution)/shard_map/update/pallas_call | solution.py:445

commit v4 on v3

--- a/solution.py
+++ b/solution.py
@@ -248,14 +248,12 @@
         widen(wide0, got0, 2 * zz + 1 - h)
     unpack(wide0, X0)
 
-    both = dot_nt(rows[:X2], rows[X0:X2])
-    mine = turned[LANE1:, : 2 * M]
-    by_field = exact(mine, both[:STEPS], ((1,), (1,)))
-    by_modes = exact(exact(mine, both[STEPS:], ((1,), (1,))), chosen[: 2 * M])
-    put(
-        part01,
-        [by_field[:, :LANES], jnp.concatenate([by_field[:, LANES:], by_modes[:, LANE1:]], axis=1)],
-    )
+    samples = rows[X0:X2]
+    by_field = dot_nt(samples, rows[:STEPS])
+    by_modes = exact(dot_nt(samples, samples), chosen[: 2 * M])
+    ends = jnp.concatenate([by_field[:, LANES:], by_modes[:, LANE1:]], axis=1)
+    both = exact(turned[LANE1:, : 2 * M], jnp.concatenate([by_field[:, :LANES], ends], axis=1))
+    put(part01, [both[:, :LANES], both[:, LANES:]])
 
     core = lax.rem(me_s, 2)
     chip = me_s // 2
@@ -342,8 +340,9 @@
     return jnp.concatenate([jnp.concatenate(row, axis=1) for row in done], axis=0)
 
 
-def update(sums, chosen, among, rows, record, out_hbm, field, out, weights, held, load_sem, store_sem):
+def update(sums, chosen, among, rows, record, out_hbm, field, out, weights, held, done, early, last, load_sem, store_sem):
     live = lax.axis_index("tm") >= 0
+    at1, at0, at2 = LANES + LANE1, LANES + LANE0, 2 * LANES
 
     load = pltpu.make_async_copy(record, field, load_sem)
     load.start()
@@ -358,34 +357,44 @@
             blocks.append(jnp.concatenate([left, right, exact(by_field, among[...])], axis=1))
         for level in range(3):
             held[level] = blocks[level]
-
-    @pl.when(live)
-    def _():
-        blocks = [held[level] for level in range(3)]
-        at1, at0, at2 = LANES + LANE1, LANES + LANE0, 2 * LANES
-
-        def change(level, done, at):
-            cols = slice(at, at + R)
-            return exact(blocks[level][:, cols] + EPS * done[:, cols], done, ((0,), (0,)))
-
-        done0 = solve(blocks[0], at0)
-        blocks[1] = blocks[1] - change(0, done0, at1)
-        blocks[2] = blocks[2] - change(0, done0, at2)
-        done1 = solve(blocks[1], at1)
-        blocks[2] = blocks[2] - change(1, done1, at2)
+        done[0] = solve(blocks[0], at0)
+
+    def change(block, done, at):
+        cols = slice(at, at + R)
+        return exact(block[:, cols] + EPS * done[:, cols], done, ((0,), (0,)))
+
+    @pl.when(live)
+    def _():
+        held[1] = held[1] - change(held[0], done[0], at1)
+
+    @pl.when(live)
+    def _():
+        held[2] = held[2] - change(held[0], done[0], at2)
+        done[1] = solve(held[1], at1)
+
+    @pl.when(live)
+    def _():
+        held[2] = held[2] - change(held[1], done[1], at2)
+
+    @pl.when(live)
+    def _():
         pick0 = chosen[:M, LANE0 : LANE0 + R]
         pick1 = chosen[M : 2 * M, LANE1 : LANE1 + R]
-        pick2 = chosen[2 * M :, :R]
-        way0 = pick0
+        done0, done1 = done[0], done[1]
         way1 = -exact(pick0, done0[:, at1 : at1 + R])
         way2 = -exact(pick0, done0[:, at2 : at2 + R]) - exact(way1, done1[:, at2 : at2 + R])
         low2 = -exact(pick1, done1[:, at2 : at2 + R])
-        part0 = exact(done0[:, :STEPS], way0, ((0,), (1,))) + exact(done1[:, :STEPS], way1, ((0,), (1,)))
+        part0 = exact(done0[:, :STEPS], pick0, ((0,), (1,))) + exact(done1[:, :STEPS], way1, ((0,), (1,)))
         part1 = exact(done1[:, :STEPS], pick1, ((0,), (1,)))
-        last = jnp.concatenate([way2, low2, pick2], axis=0)
-        early = jnp.concatenate([part0, part1, jnp.zeros((STEPS, 2 * M), jnp.float32)], axis=1)
-        done2 = solve(blocks[2], at2)
-        slopes = early + exact(done2[:, :STEPS], last, ((0,), (1,)))
+        last[: 2 * M] = jnp.concatenate([way2, low2], axis=0)
+        last[2 * M :] = chosen[2 * M :, :R]
+        early[:, : 2 * M] = jnp.concatenate([part0, part1], axis=1)
+        early[:, 2 * M :] = jnp.zeros((STEPS, 2 * M), jnp.float32)
+        done[2] = solve(held[2], at2)
+
+    @pl.when(live)
+    def _():
+        slopes = early[...] + exact(done[2][:, :STEPS], last[...], ((0,), (1,)))
         high = slopes.astype(jnp.bfloat16)
         weights[:STEPS] = high
         weights[STEPS:] = (slopes - high.astype(jnp.float32)).astype(jnp.bfloat16)
@@ -452,6 +461,9 @@
             pltpu.VMEM((STEPS, POINTS), jnp.float32),
             pltpu.VMEM((2 * STEPS, 4 * M), jnp.bfloat16),
             pltpu.VMEM((3, R, 3 * LANES), jnp.float32),
+            pltpu.VMEM((3, R, 3 * LANES), jnp.float32),
+            pltpu.VMEM((STEPS, 4 * M), jnp.float32),
+            pltpu.VMEM((4 * M, R), jnp.float32),
             dma(()), dma((POINTS // WIDTH,)),
         ],
         compiler_params=pltpu.CompilerParams(vmem_limit_bytes=VMEM_LIMIT),

time: 37.4 us -> 36.7 us (0.981)
  Pallas kernels: 37.3 us -> 36.7 us
    pallas_call x1, Pallas kernels: 31.5 us -> 30.9 us  [body(): pl.pallas_call(collect, out_shape=[pltpu.VMEM((ALL, POINTS), jnp.bfloat16...]
where the time goes in v4:
time: 36.7 us
  Pallas kernels  36.7 us (100%)
    pallas_call x1, Pallas kernels, body(): pl.pallas_call(collect, out_shape=[pltpu.VMEM((ALL, POINTS), jnp.bfloat16...  30.9 us
    pallas_call x1, Pallas kernels, body(): pl.pallas_call(update, out_shape=jax.ShapeDtypeStruct((STEPS, POINTS), jn...  5.8 us

profile of v4, /device:TPU:1, one launch (start us, length us, event | category | flops | bytes accessed | tf_op | source)
XLA Modules:
  0.0 36.7 jit_solution(2055806663335046664)
XLA Ops:
  0.0 30.9 %collect.1 = (bf16[384,4096]{1,0:T(8,128)(2,1)S(1)}, f32[24,8,128]{2,1,0:T(8,128)S(1)}, f32[192,128]{1,0:T(8,128)S(1)}, f32[192,128]{1,0:T(8,128)S(1)}) custom-call(s32[21]{0:T(128)} %phases_hbm.1, s32[21,32]{1,0:T(8,128)} %picks_hbm.1, f32[21,48,48]{2,1,0:T(8,128)} %basis_hbm.1, f32[3,4,2,256,128]{4,3,2,1,0:T(8,128)} %bitcast.5), custom_call_target="tpu_custom_call" | custom-call | tf_op jit(solution)/shard_map/collect/pallas_call | solution.py:422
  30.9 5.8 %update.1 = f32[192,4096]{1,0:T(8,128)} custom-call(f32[24,8,128]{2,1,0:T(8,128)S(1)} %get-tuple-element.9.sums, f32[192,128]{1,0:T(8,128)S(1)} %get-tuple-element.10.chosen, f32[192,128]{1,0:T(8,128)S(1)} %get-tuple-element.11.among, bf16[384,4096]{1,0:T(8,128)(2,1)S(1)} %get-tuple-element.12.rows, f32[192,4096]{1,0:T(8,128)} %record.1), custom_call_target="tpu_custom_call" | custom-call | tf_op jit(solution)/shard_map/update/pallas_call | solution.py:454

commit v5 on v4

--- a/solution.py
+++ b/solution.py
@@ -32,7 +32,6 @@
 ALL = X2 + 2 * M
 LANE1 = 64
 LANE0 = 96
-OWNERS2 = 8
 
 
 def dot_nt(a, b):
@@ -47,22 +46,28 @@
     phases_hbm, picks_hbm, basis_hbm, record,
     rows, sums, chosen, among,
     phases, picks, head, field_even, field_odd, got0, got1, wide0, wide1, basis, turned, pad,
-    part2, inbox2, total2, part01, inbox_mate, halves, total01,
+    part2, inbox2, halves2, total2, part01, inbox01, halves01, total01,
     load_sem, small_sem, recv0_sem, sem,
 ):
     send0_sem, sendy_sem, recvy_sem, send1_sem, recv1_sem = [sem.at[i] for i in range(5)]
-    recvp_sem = sem.at[15]
-    sems2 = [sem.at[i] for i in range(5, 9)]
-    mate_sems, chip_sems, back_sems = [[sem.at[j], sem.at[j + 1]] for j in (9, 11, 13)]
+    sems2, sems01 = [[sem.at[i] for i in range(j, j + 6)] for j in (5, 11)]
+    recvp_sem, late_sem = sem.at[17], sem.at[18]
     me_t = lax.axis_index("tm")
     me_s = lax.axis_index("space")
+    core = lax.rem(me_s, 2)
     first = me_t // GROUP * GROUP
 
     barrier = pltpu.get_barrier_semaphore()
-    for d in range(1, NT):
+    for d in range(2, NT, 2):
         pl.semaphore_signal(barrier, inc=1, device_id={"tm": lax.rem(me_t + d, NT)}, device_id_type=MESH)
-    for d in range(1, NS):
-        pl.semaphore_signal(barrier, inc=1, device_id={"space": lax.rem(me_s + d, NS)}, device_id_type=MESH)
+    partner = me_t + 1 - 2 * lax.rem(me_t, 2)
+    pl.semaphore_signal(barrier, inc=1, device_id={"tm": partner}, device_id_type=MESH)
+    chip = me_s // 2
+    mate = me_s + 1 - 2 * core
+    for d in range(1, CHIPS):
+        peer = 2 * lax.rem(chip + d, CHIPS) + core
+        pl.semaphore_signal(barrier, inc=1, device_id={"space": peer}, device_id_type=MESH)
+    pl.semaphore_signal(barrier, inc=1, device_id={"space": mate}, device_id_type=MESH)
 
     get_phases = pltpu.make_async_copy(phases_hbm, phases, small_sem.at[3])
     get_phases.start()
@@ -92,11 +97,10 @@
     for r in range(ROWS0):
         got0[me_t, r * SEGS : (r + 1) * SEGS] = head[pl.ds(r * BLOCK + off0, SEGS, stride=8), :].astype(jnp.bfloat16)
 
-    pl.semaphore_wait(barrier, NT - 1 + NS - 1)
+    pl.semaphore_wait(barrier, NZ + CHIPS)
 
     z = me_t // 2
     h = lax.rem(me_t, 2)
-    partner = me_t + 1 - 2 * h
     near = me_t + 2 - 4 * lax.rem(z, 2)
     across = near + 1 - 2 * h
 
@@ -124,7 +128,7 @@
     turn = [lax.rem(z + d + NZ, NZ) for d in hops]
     out0 = [along0(2 * turn[i] + h, me_t, send0_sem, recv0_sem.at[z]) for i in range(7)]
     in0 = [along0(2 * turn[i] + h, 2 * turn[i] + h, send0_sem, recv0_sem.at[turn[i]]) for i in range(7)]
-    over0 = [along0(partner, 2 * turn[i] + h, sendy_sem, recvy_sem) for i in range(7)]
+    over0 = [along0(partner, 2 * turn[i] + h, sendy_sem, recvy_sem if i < 4 else late_sem) for i in range(7)]
     over0.append(along0(partner, me_t, sendy_sem, recvy_sem))
     peers1 = (near, partner, across)
     out1 = [along1(near, me_t, recv1_sem), along1(partner, me_t, recvp_sem), along1(near, partner, recv1_sem)]
@@ -202,18 +206,49 @@
     by_field2 = exact(turned[:R, 2 * M :], dot_nt(rows[:STEPS], rows[X2:]), ((1,), (1,)))
     put(part2, [by_field2[:, :LANES], jnp.concatenate([by_field2[:, LANES:], space], axis=1)])
 
-    def others(do):
-        pl.when(me_s < OWNERS2)(lambda: do(OWNERS2 - 1))
-        pl.when(me_s >= OWNERS2)(lambda: do(OWNERS2))
-
-    for d in range(1, NS):
-        tgt = lax.rem(me_s + d, NS)
-        copy = pltpu.make_async_remote_copy(
-            src_ref=part2.at[lax.rem(tgt, OWNERS2)], dst_ref=inbox2.at[me_s],
-            send_sem=sems2[0], recv_sem=sems2[1],
-            device_id={"space": tgt}, device_id_type=MESH,
+    def to_mate(src, dst, sems):
+        return pltpu.make_async_remote_copy(
+            src_ref=src, dst_ref=dst, send_sem=sems[0], recv_sem=sems[1],
+            device_id={"space": mate}, device_id_type=MESH,
         )
-        pl.when(tgt < OWNERS2)(copy.start)
+
+    class Sum:
+        def __init__(self, part, inbox, halves, total, sems):
+            self.part, self.inbox, self.halves, self.total, self.sems = part, inbox, halves, total, sems
+            count = inbox.shape[0]
+            self.mine = pl.ds(core * count, count)
+            self.give = to_mate(part.at[pl.ds(count - core * count, count)], inbox, sems[:2])
+            self.back = to_mate(total.at[self.mine], total.at[self.mine], sems[4:])
+
+        def swap(self):
+            self.give.wait_recv()
+            self.halves[chip] = self.part[self.mine] + self.inbox[...]
+            for d in range(1, CHIPS):
+                pltpu.make_async_remote_copy(
+                    src_ref=self.halves.at[chip], dst_ref=self.halves.at[chip],
+                    send_sem=self.sems[2], recv_sem=self.sems[3],
+                    device_id={"space": 2 * lax.rem(chip + d, CHIPS) + core}, device_id_type=MESH,
+                ).start()
+
+        def add(self):
+            self.swapped().wait_recv()
+            acc = self.halves[0]
+            for i in range(1, CHIPS):
+                acc = acc + self.halves[i]
+            self.total[self.mine] = acc
+            self.back.start()
+
+        def swapped(self):
+            return whole(self.halves, CHIPS - 1, self.sems[2], self.sems[3])
+
+        def settle(self):
+            self.give.wait_send()
+            self.swapped().wait_send()
+            self.back.wait_send()
+
+    sum2 = Sum(part2, inbox2, halves2, total2, sems2)
+    sum01 = Sum(part01, inbox01, halves01, total01, sems01)
+    sum2.give.start()
 
     for i in range(7):
         pass0(i)
@@ -221,19 +256,7 @@
             in_partner.wait_recv()
             out1[2].start()
 
-    @pl.when(me_s < OWNERS2)
-    def _():
-        own = lax.rem(me_s, OWNERS2)
-        whole(inbox2, NS - 1, sems2[0], sems2[1]).wait_recv()
-        acc = part2[own]
-        for d in range(1, NS):
-            acc = acc + inbox2[lax.rem(me_s + d, NS)]
-        total2[own] = acc
-        for d in range(1, NS):
-            pltpu.make_async_remote_copy(
-                src_ref=total2.at[own], dst_ref=total2.at[own], send_sem=sems2[2], recv_sem=sems2[3],
-                device_id={"space": lax.rem(me_s + d, NS)}, device_id_type=MESH,
-            ).start()
+    sum2.swap()
 
     def unpack(wide, at):
         for j in range(SEGS):
@@ -243,8 +266,11 @@
     for peer in peers1:
         widen(wide1, got1, peer - first)
     unpack(wide1, X1)
-    whole(got0, NZ, sendy_sem, recvy_sem).wait_recv()
-    for zz in (*turn, z):
+    whole(got0, 5, sendy_sem, recvy_sem).wait_recv()
+    for zz in (*turn[:4], z):
+        widen(wide0, got0, 2 * zz + 1 - h)
+    whole(got0, 3, sendy_sem, late_sem).wait_recv()
+    for zz in turn[4:]:
         widen(wide0, got0, 2 * zz + 1 - h)
     unpack(wide0, X0)
 
@@ -255,46 +281,20 @@
     both = exact(turned[LANE1:, : 2 * M], jnp.concatenate([by_field[:, :LANES], ends], axis=1))
     put(part01, [both[:, :LANES], both[:, LANES:]])
 
-    core = lax.rem(me_s, 2)
-    chip = me_s // 2
-    mate = me_s + 1 - 2 * core
-    mine = pl.ds(core * 8, 8)
-
-    def to_mate(src, dst, sems):
-        return pltpu.make_async_remote_copy(
-            src_ref=src, dst_ref=dst, send_sem=sems[0], recv_sem=sems[1],
-            device_id={"space": mate}, device_id_type=MESH,
-        )
-
-    give = to_mate(part01.at[pl.ds(8 - core * 8, 8)], inbox_mate, mate_sems)
-    give.start()
-    give.wait_recv()
-    halves[chip] = part01[mine] + inbox_mate[...]
-    for d in range(1, CHIPS):
-        pltpu.make_async_remote_copy(
-            src_ref=halves.at[chip], dst_ref=halves.at[chip], send_sem=chip_sems[0], recv_sem=chip_sems[1],
-            device_id={"space": 2 * lax.rem(chip + d, CHIPS) + core}, device_id_type=MESH,
-        ).start()
-    whole(halves, CHIPS - 1, chip_sems[0], chip_sems[1]).wait_recv()
-    acc = halves[0]
-    for i in range(1, CHIPS):
-        acc = acc + halves[i]
-    total01[mine] = acc
-    back = to_mate(total01.at[mine], total01.at[mine], back_sems)
-    back.start()
-    others(lambda count: whole(total2, count, sems2[2], sems2[3]).wait_recv())
+    sum01.give.start()
+    sum2.add()
+    sum01.swap()
+    sum01.add()
+    sum2.back.wait_recv()
     sums[16:] = total2[...]
-    back.wait_recv()
+    sum01.back.wait_recv()
     sums[:16] = total01[...]
 
     whole(got0, NZ - 1, send0_sem, recv0_sem.at[z]).wait_send()
     whole(got0, NZ, sendy_sem, recvy_sem).wait_send()
     whole(got1, GROUP - 1, send1_sem, recv1_sem).wait_send()
-    others(lambda count: whole(inbox2, count, sems2[0], sems2[1]).wait_send())
-    pl.when(me_s < OWNERS2)(whole(inbox2, NS - 1, sems2[2], sems2[3]).wait_send)
-    give.wait_send()
-    whole(halves, CHIPS - 1, chip_sems[0], chip_sems[1]).wait_send()
-    back.wait_send()
+    sum2.settle()
+    sum01.settle()
 
 
 def eliminate(tiles, pivot_tile, pivot_lane):
@@ -370,6 +370,13 @@
     @pl.when(live)
     def _():
         held[2] = held[2] - change(held[0], done[0], at2)
+        pick0 = chosen[:M, LANE0 : LANE0 + R]
+        done0 = done[0]
+        way1 = -exact(pick0, done0[:, at1 : at1 + R])
+        last[M : 2 * M] = way1
+        last[:M] = -exact(pick0, done0[:, at2 : at2 + R])
+        early[:, :M] = exact(done0[:, :STEPS], pick0, ((0,), (1,)))
+        early[:, 2 * M :] = jnp.zeros((STEPS, 2 * M), jnp.float32)
         done[1] = solve(held[1], at1)
 
     @pl.when(live)
@@ -378,18 +385,15 @@
 
     @pl.when(live)
     def _():
-        pick0 = chosen[:M, LANE0 : LANE0 + R]
         pick1 = chosen[M : 2 * M, LANE1 : LANE1 + R]
-        done0, done1 = done[0], done[1]
-        way1 = -exact(pick0, done0[:, at1 : at1 + R])
-        way2 = -exact(pick0, done0[:, at2 : at2 + R]) - exact(way1, done1[:, at2 : at2 + R])
-        low2 = -exact(pick1, done1[:, at2 : at2 + R])
-        part0 = exact(done0[:, :STEPS], pick0, ((0,), (1,))) + exact(done1[:, :STEPS], way1, ((0,), (1,)))
-        part1 = exact(done1[:, :STEPS], pick1, ((0,), (1,)))
-        last[: 2 * M] = jnp.concatenate([way2, low2], axis=0)
+        done1 = done[1]
+        way1 = last[M : 2 * M]
+        by_field1 = done1[:, :STEPS]
+        early[:, :M] = early[:, :M] + exact(by_field1, way1, ((0,), (1,)))
+        early[:, M : 2 * M] = exact(by_field1, pick1, ((0,), (1,)))
+        last[:M] = last[:M] - exact(way1, done1[:, at2 : at2 + R])
+        last[M : 2 * M] = -exact(pick1, done1[:, at2 : at2 + R])
         last[2 * M :] = chosen[2 * M :, :R]
-        early[:, : 2 * M] = jnp.concatenate([part0, part1], axis=1)
-        early[:, 2 * M :] = jnp.zeros((STEPS, 2 * M), jnp.float32)
         done[2] = solve(held[2], at2)
 
     @pl.when(live)
@@ -442,8 +446,8 @@
             pltpu.VMEM((3, M, M), jnp.float32),
             pltpu.VMEM((LANES, 4 * M), jnp.float32),
             pltpu.VMEM((M, LANES), jnp.float32),
-            chunk(8), chunk(NS), chunk(8), chunk(16), chunk(8), chunk(CHIPS, 8), chunk(16),
-            dma((3,)), dma((5,)), dma((NZ,)), dma((16,)),
+            chunk(8), chunk(4), chunk(CHIPS, 4), chunk(8), chunk(16), chunk(8), chunk(CHIPS, 8), chunk(16),
+            dma((3,)), dma((5,)), dma((NZ,)), dma((19,)),
         ],
         compiler_params=pltpu.CompilerParams(
             collective_id=0, has_side_effects=True, vmem_limit_bytes=VMEM_LIMIT

time: 36.7 us -> 36.1 us (0.984)
  Pallas kernels: 36.7 us -> 36 us
    pallas_call x1, Pallas kernels: 30.9 us -> 30.3 us  [body(): pl.pallas_call(collect, out_shape=[pltpu.VMEM((ALL, POINTS), jnp.bfloat16...]
where the time goes in v5:
time: 36.1 us; the launch traced here: 36 us
  Pallas kernels  36 us (100%)
    pallas_call x1, Pallas kernels, body(): pl.pallas_call(collect, out_shape=[pltpu.VMEM((ALL, POINTS), jnp.bfloat16...  30.3 us
    pallas_call x1, Pallas kernels, body(): pl.pallas_call(update, out_shape=jax.ShapeDtypeStruct((STEPS, POINTS), jn...  5.7 us

profile of v5, /device:TPU:1, one launch (start us, length us, event | category | flops | bytes accessed | tf_op | source)
XLA Modules:
  0.0 36.0 jit_solution(2240700247445868086)
XLA Ops:
  0.0 30.3 %collect.1 = (bf16[384,4096]{1,0:T(8,128)(2,1)S(1)}, f32[24,8,128]{2,1,0:T(8,128)S(1)}, f32[192,128]{1,0:T(8,128)S(1)}, f32[192,128]{1,0:T(8,128)S(1)}) custom-call(s32[21]{0:T(128)} %phases_hbm.1, s32[21,32]{1,0:T(8,128)} %picks_hbm.1, f32[21,48,48]{2,1,0:T(8,128)} %basis_hbm.1, f32[3,4,2,256,128]{4,3,2,1,0:T(8,128)} %bitcast.5), custom_call_target="tpu_custom_call" | custom-call | tf_op jit(solution)/shard_map/collect/pallas_call | solution.py:426
  30.3 5.7 %update.1 = f32[192,4096]{1,0:T(8,128)} custom-call(f32[24,8,128]{2,1,0:T(8,128)S(1)} %get-tuple-element.9.sums, f32[192,128]{1,0:T(8,128)S(1)} %get-tuple-element.10.chosen, f32[192,128]{1,0:T(8,128)S(1)} %get-tuple-element.11.among, bf16[384,4096]{1,0:T(8,128)(2,1)S(1)} %get-tuple-element.12.rows, f32[192,4096]{1,0:T(8,128)} %record.1), custom_call_target="tpu_custom_call" | custom-call | tf_op jit(solution)/shard_map/update/pallas_call | solution.py:458

commit v6 on v5

--- a/solution.py
+++ b/solution.py
@@ -140,8 +140,7 @@
         got1[me_t - first, r * SEGS : (r + 1) * SEGS] = field_even[
             pl.ds(r * BLOCK + off1, SEGS, stride=8), :
         ].astype(jnp.bfloat16)
-    for copy in (out1[1], out1[0]):
-        copy.start()
+    out1[1].start()
 
     def widen(wide, got, slot):
         count = got.shape[1] // SEGS
@@ -252,6 +251,8 @@
 
     for i in range(7):
         pass0(i)
+        if i == 1:
+            out1[0].start()
         if i == 3:
             in_partner.wait_recv()
             out1[2].start()
@@ -282,8 +283,8 @@
     put(part01, [both[:, :LANES], both[:, LANES:]])
 
     sum01.give.start()
+    sum01.swap()
     sum2.add()
-    sum01.swap()
     sum01.add()
     sum2.back.wait_recv()
     sums[16:] = total2[...]

time: 36.1 us -> 35.9 us (level)
  no operation moved by 1% of the time
where the time goes in v6:
time: 35.9 us; the launch traced here: 35.8 us
  Pallas kernels  35.8 us (100%)
    pallas_call x1, Pallas kernels, body(): pl.pallas_call(collect, out_shape=[pltpu.VMEM((ALL, POINTS), jnp.bfloat16...  30.1 us
    pallas_call x1, Pallas kernels, body(): pl.pallas_call(update, out_shape=jax.ShapeDtypeStruct((STEPS, POINTS), jn...  5.71 us

profile of v6, /device:TPU:1, one launch (start us, length us, event | category | flops | bytes accessed | tf_op | source)
XLA Modules:
  0.0 35.8 jit_solution(5621818471514520865)
XLA Ops:
  0.0 30.1 %collect.1 = (bf16[384,4096]{1,0:T(8,128)(2,1)S(1)}, f32[24,8,128]{2,1,0:T(8,128)S(1)}, f32[192,128]{1,0:T(8,128)S(1)}, f32[192,128]{1,0:T(8,128)S(1)}) custom-call(s32[21]{0:T(128)} %phases_hbm.1, s32[21,32]{1,0:T(8,128)} %picks_hbm.1, f32[21,48,48]{2,1,0:T(8,128)} %basis_hbm.1, f32[3,4,2,256,128]{4,3,2,1,0:T(8,128)} %bitcast.5), custom_call_target="tpu_custom_call" | custom-call | tf_op jit(solution)/shard_map/collect/pallas_call | solution.py:427
  30.1 5.7 %update.1 = f32[192,4096]{1,0:T(8,128)} custom-call(f32[24,8,128]{2,1,0:T(8,128)S(1)} %get-tuple-element.9.sums, f32[192,128]{1,0:T(8,128)S(1)} %get-tuple-element.10.chosen, f32[192,128]{1,0:T(8,128)S(1)} %get-tuple-element.11.among, bf16[384,4096]{1,0:T(8,128)(2,1)S(1)} %get-tuple-element.12.rows, f32[192,4096]{1,0:T(8,128)} %record.1), custom_call_target="tpu_custom_call" | custom-call | tf_op jit(solution)/shard_map/update/pallas_call | solution.py:459

commit v7 on v6

--- a/solution.py
+++ b/solution.py
@@ -72,7 +72,7 @@
     get_phases = pltpu.make_async_copy(phases_hbm, phases, small_sem.at[3])
     get_phases.start()
     load_even, load_odd = [
-        pltpu.make_async_copy(record.at[:, :, i], half.reshape(ROWS0, ROWS1 // ROWS0, BLOCK, LANES), load_sem.at[i])
+        pltpu.make_async_copy(record.at[:, :, i], half.reshape(ROWS0 + 1, ROWS1 // ROWS0, BLOCK, LANES).at[pl.ds(0, ROWS0)], load_sem.at[i])
         for i, half in enumerate((field_even, field_odd))
     ]
     load_head = pltpu.make_async_copy(record.at[:, 0, 0], head.reshape(ROWS0, BLOCK, LANES), load_sem.at[2])
@@ -187,7 +187,7 @@
         spots = jnp.concatenate([*none(place), picks[pl.ds(q, 1), :], *none(3 - place)], axis=1)
         columns = exact(basis[level], (row_m == spots).astype(jnp.float32))
         if level == 2:
-            pad[...] = columns
+            pad[:M] = columns
             columns = jnp.concatenate([pad[pl.ds(i, M // 4, stride=4), :] for i in range(4)], axis=0)
             chosen[3 * M :] = columns
         chosen[at : at + M] = columns
@@ -438,15 +438,15 @@
             pltpu.SMEM((21,), jnp.int32),
             pltpu.VMEM((21, R), jnp.int32),
             pltpu.VMEM((ROWS0 * BLOCK, LANES), jnp.float32),
-            pltpu.VMEM((TILES // 2 * BLOCK, LANES), jnp.float32),
-            pltpu.VMEM((TILES // 2 * BLOCK, LANES), jnp.float32),
+            pltpu.VMEM(((ROWS1 + ROWS1 // ROWS0) * BLOCK, LANES), jnp.float32),
+            pltpu.VMEM(((ROWS1 + ROWS1 // ROWS0) * BLOCK, LANES), jnp.float32),
             pltpu.VMEM((NT, ROWS0 * SEGS, LANES), jnp.bfloat16),
             pltpu.VMEM((GROUP, ROWS1 * SEGS, LANES), jnp.bfloat16),
             pltpu.VMEM((M * SEGS, LANES), jnp.float32),
             pltpu.VMEM((M * SEGS, LANES), jnp.float32),
             pltpu.VMEM((3, M, M), jnp.float32),
             pltpu.VMEM((LANES, 4 * M), jnp.float32),
-            pltpu.VMEM((M, LANES), jnp.float32),
+            pltpu.VMEM((M + 16, LANES), jnp.float32),
             chunk(8), chunk(4), chunk(CHIPS, 4), chunk(8), chunk(16), chunk(8), chunk(CHIPS, 8), chunk(16),
             dma((3,)), dma((5,)), dma((NZ,)), dma((19,)),
         ],

time: 35.9 us -> 35.9 us (level)
  no operation moved by 1% of the time
where the time goes in v7:
time: 35.9 us; the launch traced here: 35.8 us
  Pallas kernels  35.8 us (100%)
    pallas_call x1, Pallas kernels, body(): pl.pallas_call(collect, out_shape=[pltpu.VMEM((ALL, POINTS), jnp.bfloat16...  30.1 us
    pallas_call x1, Pallas kernels, body(): pl.pallas_call(update, out_shape=jax.ShapeDtypeStruct((STEPS, POINTS), jn...  5.71 us

profile of v7, /device:TPU:1, one launch (start us, length us, event | category | flops | bytes accessed | tf_op | source)
XLA Modules:
  0.0 35.8 jit_solution(3578114353096953840)
XLA Ops:
  0.0 30.1 %collect.1 = (bf16[384,4096]{1,0:T(8,128)(2,1)S(1)}, f32[24,8,128]{2,1,0:T(8,128)S(1)}, f32[192,128]{1,0:T(8,128)S(1)}, f32[192,128]{1,0:T(8,128)S(1)}) custom-call(s32[21]{0:T(128)} %phases_hbm.1, s32[21,32]{1,0:T(8,128)} %picks_hbm.1, f32[21,48,48]{2,1,0:T(8,128)} %basis_hbm.1, f32[3,4,2,256,128]{4,3,2,1,0:T(8,128)} %bitcast.5), custom_call_target="tpu_custom_call" | custom-call | tf_op jit(solution)/shard_map/collect/pallas_call | solution.py:427
  30.1 5.7 %update.1 = f32[192,4096]{1,0:T(8,128)} custom-call(f32[24,8,128]{2,1,0:T(8,128)S(1)} %get-tuple-element.9.sums, f32[192,128]{1,0:T(8,128)S(1)} %get-tuple-element.10.chosen, f32[192,128]{1,0:T(8,128)S(1)} %get-tuple-element.11.among, bf16[384,4096]{1,0:T(8,128)(2,1)S(1)} %get-tuple-element.12.rows, f32[192,4096]{1,0:T(8,128)} %record.1), custom_call_target="tpu_custom_call" | custom-call | tf_op jit(solution)/shard_map/update/pallas_call | solution.py:459
